TPU v7x, 128 devices: a whole 4x4x4 slice. The times are simulated.
128 devices in a mesh: tm: 32 (over y, x, core), cluster: 4 (over z).
Axes of the slice: x: 4, y: 4, z: 4, core: 2. Of those that a mesh axis runs over, the one named last changes fastest.
Arguments:
- cotangent: bfloat16 [32, 12288, 512], P(None, ('cluster', 'tm')), may hold values from -6 to 6
- propagated: bfloat16 [32, 12288, 512], P('tm', 'cluster'), may hold values from -0.0546875 to 0.0546875
- weight: bfloat16 [32, 512, 512], P('tm'), may hold values from -0.25 to 0.25
- block_rows: int32 [32, 4, 128], P('tm', 'cluster'), may hold values from 0 to 23
- block_cols: int32 [32, 4, 128], P('tm', 'cluster'), may hold values from 0 to 23
- block_values: bfloat16 [32, 4, 128, 128, 128], P('tm', 'cluster'), may hold values from -0.21875 to 0.21875
- block_counts: int32 [32, 4], P('tm', 'cluster'), may hold values from 1 to 128, as said below
- band: int32 [32], replicated, may hold values from 1 to 4, as said below
Outputs:
- input_grad: bfloat16 [32, 12288, 512], P(None, ('cluster', 'tm'))
- weight_grad: float32 [32, 512, 512], P('tm')
Inputs may be any that keep to these rules, and one draw needn't show every extreme that they name: `block_counts`: slots past the count are ignored; the last snapshot has 128 live blocks in some cluster. Some snapshot has band width 4.
All inputs are finite; a program needn't handle non-finite values.
Results may differ from a plain program's by a relative error of at most 0.014.
Values may be sent and summed in bfloat16 or wider, within the bound.
No kernel may reach another device: no remote copies, remote signals or barrier semaphores. Data moves between devices by JAX's collectives and lax.ppermute only.
A program may use at most 192 MiB of HBM per device.

v0:
```python
import jax
import jax.numpy as jnp
from jax import lax
from jax.sharding import PartitionSpec as P

BAND = 4


def band_weights(band):
    total = band.shape[0]
    start = jnp.arange(total, dtype=jnp.int32)[:, None]
    offset = jnp.arange(BAND, dtype=jnp.int32)[None, :]
    target = start + offset
    widths = band[jnp.minimum(target, total - 1)]
    valid = (target < total) & (offset < widths)
    return jnp.where(valid, 1.0 / widths.astype(jnp.float32), 0.0)


def local_band(field, weights):
    result = weights[:, 0][:, None, None] * field
    for offset in range(1, BAND):
        later = jnp.concatenate(
            [field[offset:], jnp.zeros((offset,) + field.shape[1:], field.dtype)], axis=0
        )
        result = result + weights[:, offset][:, None, None] * later
    return result


def to_snapshots(field):
    return lax.all_to_all(field, "tm", split_axis=0, concat_axis=1, tiled=True)


def to_vertices(field):
    return lax.all_to_all(field, "tm", split_axis=1, concat_axis=0, tiled=True)


def transposed_hop(feats, rows, cols, values, count):
    row_tiles = feats.shape[0] // 128
    width = feats.shape[1]
    tiles = feats.reshape(row_tiles, 128, width)
    tile_ids = jnp.arange(row_tiles, dtype=jnp.int32)[None, :]
    rows_hot = (rows[:, None] == tile_ids).astype(jnp.bfloat16)
    picked = jnp.einsum("br,rif->bif", rows_hot, tiles, preferred_element_type=jnp.float32).astype(
        jnp.bfloat16
    )
    prod = jnp.einsum("bij,bif->bjf", values, picked, preferred_element_type=jnp.float32)
    live = jnp.arange(rows.shape[0], dtype=jnp.int32) < count
    cols_hot = ((cols[:, None] == tile_ids) & live[:, None]).astype(jnp.float32)
    result = jnp.einsum(
        "bk,bjf->kjf",
        cols_hot,
        prod,
        precision=lax.Precision.HIGHEST,
        preferred_element_type=jnp.float32,
    )
    return result.reshape(row_tiles * 128, width)


def on_device(
    cotangent, propagated, weight, block_rows, block_cols, block_values, block_counts, band
):
    weights = band_weights(band)
    dz = to_snapshots(local_band(cotangent, weights).astype(jnp.bfloat16))[0]
    terms = jnp.einsum("vf,vg->fg", propagated[0], dz, preferred_element_type=jnp.float32)
    weight_grad = lax.psum(terms.astype(jnp.bfloat16), "cluster").astype(jnp.float32)
    pushed = jnp.einsum("vg,fg->vf", dz, weight[0], preferred_element_type=jnp.float32).astype(
        jnp.bfloat16
    )
    rows = block_rows[0, 0]
    cols = block_cols[0, 0]
    values = block_values[0, 0]
    count = block_counts[0, 0]
    first = transposed_hop(pushed, rows, cols, values, count).astype(jnp.bfloat16)
    second = transposed_hop(first, rows, cols, values, count).astype(jnp.bfloat16)[None]
    input_grad = local_band(to_vertices(second), weights).astype(jnp.bfloat16)
    return (input_grad, weight_grad[None])


def solution(mesh):
    placed = (
        P(None, ("cluster", "tm"), None),
        P("tm", "cluster", None),
        P("tm", None, None),
        P("tm", "cluster", None),
        P("tm", "cluster", None),
        P("tm", "cluster", None, None, None),
        P("tm", "cluster"),
        P(),
    )
    return jax.shard_map(
        on_device,
        mesh=mesh,
        in_specs=placed,
        out_specs=(P(None, ("cluster", "tm"), None), P("tm", None, None)),
        check_vma=False,
    )
```

profile of v0, /device:TPU:0, one launch (start us, length us, event | category | flops | bytes accessed | tf_op | source)
XLA Modules:
  0.0 432.1 jit_solution(11716909796205269512)
XLA Ops:
  7.2 0.0 copy-start
  7.2 0.0 copy-start.2
  7.2 3.9 slice.49
  11.1 0.0 copy-done.2
  11.1 1.9 slice.47
  13.0 1.9 slice.45
  15.0 0.1 reshape.75
  15.1 0.0 copy-done.1
  15.1 1.2 gather_fusion
  16.3 0.1 reshape.74
  16.4 0.2 slice_reduce_fusion.3
  16.7 0.0 copy-start.5
  16.7 0.5 copy-done.3
  17.2 0.0 copy-done.5
  17.3 7.5 %add_convert_fusion.1 = bf16[32,96,512]{2,1,0:T(8,128)(2,1)} fusion(bf16[32,96,512]{2,1,0:T(8,128)(2,1)} %param.8, bf16[29,96,512]{2,1,0:T(8,128)(2,1)} %slice.49, f32[32]{0:T(128)S(1)} %get-tuple-element.11, bf16[30,96,512]{2,1,0:T(8,128)(2,1)} %slice.47, f32[32]{0:T(128)S(1)} %get-tuple-element.12, bf16[31,96,512]{2,1,0:T(8,128)(2,1)} %slice.45, ...), kind=kLoop, calls=%fused_computation.10 | loop fusion | flops 18874368 | bytes 15139328 | tf_op jit(solution)/shard_map/convert_element_type | solution.py:63
  24.8 8.0 %all-to-all-start = ((bf16[32,96,512]{2,1,0:T(8,128)(2,1)}), bf16[32,96,512]{2,1,0:T(8,128)(2,1)}, u32[]{:S(2)}, u32[]{:S(2)}) async-start(bf16[32,96,512]{2,1,0:T(8,128)(2,1)} %add_convert_fusion.1), calls=%async_computation | async-start | bytes 6291456 | tf_op jit(solution)/shard_map/all_to_all | solution.py:30
  33.5 41.1 %all-to-all-done = bf16[32,96,512]{2,1,0:T(8,128)(2,1)} async-done(((bf16[32,96,512]{2,1,0:T(8,128)(2,1)}), bf16[32,96,512]{2,1,0:T(8,128)(2,1)}, u32[]{:S(2)}, u32[]{:S(2)}) %all-to-all-start) | async-done | bytes 3145760 | tf_op jit(solution)/shard_map/all_to_all | solution.py:30
  74.6 5.5 %convolution_convert_fusion.2 = bf16[3072,512]{1,0:T(8,128)(2,1)} fusion(bf16[3072,512]{1,0:T(8,128)(2,1)} %bitcast.5, bf16[1,512,512]{2,1,0:T(8,128)(2,1)} %param.10), kind=kOutput, calls=%fused_computation.11 | convolution fusion | flops 1612185600 | bytes 6815744 | tf_op jit(solution)/shard_map/vg,fg->vf/dot_general | solution.py:66
  80.1 12.1 %convolution_convert_fusion.1 = bf16[128,128,512]{2,0,1:T(8,128)(2,1)} fusion(bf16[24,128,512]{2,1,0:T(8,128)(2,1)} %bitcast.65, s32[128]{0:T(128)S(1)} %bitcast.66), kind=kOutput, calls=%fused_computation.8 | convolution fusion | flops 411044864 | bytes 19923456 | tf_op jit(solution)/shard_map/br,rif->bif/dot_general | solution.py:43
  92.2 23.4 %fusion.4 = f32[128,128,512]{1,2,0:T(8,128)} fusion(bf16[128,128,512]{2,0,1:T(8,128)(2,1)} %convolution_convert_fusion.1, bf16[1,1,128,128,128]{4,3,2,1,0:T(8,128)(2,1)} %param.13), kind=kOutput, calls=%fused_computation.5 | convolution fusion | flops 2147483648 | bytes 54525952 | tf_op jit(solution)/shard_map/bij,bif->bjf/dot_general | solution.py:46
  115.6 34.6 %copy.23 = f32[128,128,512]{2,0,1:T(8,128)} copy(f32[128,128,512]{1,2,0:T(8,128)} %fusion.4) | data formatting | bytes 67108864 | tf_op jit(solution)/shard_map/bij,bif->bjf/dot_general | solution.py:46
  150.2 17.4 %fusion.30 = bf16[24,128,512]{2,0,1:T(8,128)(2,1)} fusion(f32[128,128,512]{2,0,1:T(8,128)} %copy.23, s32[128]{0:T(128)S(1)} %bitcast.68, pred[128]{0:T(512)(128)(4,1)S(1)} %iota_compare_fusion.3), kind=kOutput, calls=%fused_computation.36 | convolution fusion | flops 2415925248 | bytes 36700800 | tf_op jit(solution)/shard_map/bk,bjf->kjf/dot_general | solution.py:49
  167.6 12.1 %convolution_convert_fusion = bf16[128,128,512]{2,0,1:T(8,128)(2,1)} fusion(bf16[24,128,512]{2,0,1:T(8,128)(2,1)} %fusion.30, s32[128]{0:T(128)S(1)} %bitcast.67), kind=kOutput, calls=%fused_computation.7 | convolution fusion | flops 411044864 | bytes 19923456 | tf_op jit(solution)/shard_map/br,rif->bif/dot_general | solution.py:43
  179.8 23.4 %fusion.7 = f32[128,128,512]{1,2,0:T(8,128)} fusion(bf16[128,128,512]{2,0,1:T(8,128)(2,1)} %convolution_convert_fusion, bf16[1,1,128,128,128]{4,3,2,1,0:T(8,128)(2,1)} %param.13), kind=kOutput, calls=%fused_computation.6 | convolution fusion | flops 2147483648 | bytes 54525952 | tf_op jit(solution)/shard_map/bij,bif->bjf/dot_general | solution.py:46
  203.1 34.6 %copy.25 = f32[128,128,512]{2,0,1:T(8,128)} copy(f32[128,128,512]{1,2,0:T(8,128)} %fusion.7) | data formatting | bytes 67108864 | tf_op jit(solution)/shard_map/bij,bif->bjf/dot_general | solution.py:46
  237.7 17.5 %convolution_convert_fusion.3 = bf16[24,128,512]{2,0,1:T(8,128)(2,1)} fusion(f32[128,128,512]{2,0,1:T(8,128)} %copy.25, s32[128]{0:T(128)S(1)} %bitcast.69, pred[128]{0:T(512)(128)(4,1)S(1)} %iota_compare_fusion.3), kind=kOutput, calls=%fused_computation.18 | convolution fusion | flops 2417498112 | bytes 36700800 | tf_op jit(solution)/shard_map/bk,bjf->kjf/dot_general | solution.py:49
  255.2 2.9 copy.26
  258.1 27.4 %copy.47 = bf16[1,3072,512]{2,0,1:T(2,128)(2,1)} copy(bf16[1,3072,512]{2,1,0:T(8,128)(2,1)S(1)} %bitcast.61) | data formatting | bytes 6291456 | tf_op jit(solution)/shard_map/convert_element_type | solution.py:74
  285.6 0.5 broadcast.62
  286.1 21.9 %reduce.8 = bf16[3072,512]{1,0:T(8,128)(2,1)} reduce(bf16[3072,1,512]{2,1,0:T(2,128)(2,1)} %bitcast.60, bf16[]{:T(256)} %broadcast.62), dimensions={1}, to_apply=%bitcast.51.reduce_sub_computation | reduce | bytes 6291458
  308.0 8.5 %reshape.88 = bf16[32,2,24576]{2,1,0:T(2,128)(2,1)} reshape(bf16[3072,512]{1,0:T(8,128)(2,1)} %reduce.8) | data formatting | bytes 6291456
  316.5 4.8 %all-to-all-start.1 = ((bf16[32,2,24576]{2,1,0:T(2,128)(2,1)}), bf16[32,2,24576]{2,1,0:T(2,128)(2,1)}, u32[]{:S(2)}, u32[]{:S(2)}) async-start(bf16[32,2,24576]{2,1,0:T(2,128)(2,1)} %reshape.88), calls=%async_computation.1 | async-start | bytes 6291456 | tf_op jit(solution)/shard_map/all_to_all | solution.py:34
  321.3 0.3 all-reduce.8.cloned.1.call-start
  321.6 4.5 %fusion.19 = bf16[1,512,512]{1,2,0:T(8,128)(2,1)} fusion(bf16[3072,512]{1,0:T(8,128)(2,1)} %bitcast.5, bf16[1,3072,512]{2,1,0:T(8,128)(2,1)S(1)} %copy-done), kind=kOutput, calls=%fused_computation.20 | convolution fusion | flops 1610874880 | bytes 6815744 | tf_op jit(solution)/shard_map/vf,vg->fg/dot_general | solution.py:64
  326.1 0.0 all-reduce.8.cloned.1.call-update
  326.1 45.7 %all-reduce.8.cloned.1.call-done = bf16[1,512,512]{1,2,0:T(8,128)(2,1)} async-done(((bf16[1,512,512]{1,2,0:T(8,128)(2,1)}), bf16[1,512,512]{1,2,0:T(8,128)(2,1)}) %all-reduce.8.cloned.1.call-update) | async-done | bytes 524304 | tf_op jit(solution)/shard_map/psum | solution.py:65
  371.8 2.2 copy.31
  374.1 0.0 all-to-all-done.1
  374.1 18.9 %reshape.89 = bf16[3072,1,512]{2,1,0:T(2,128)(2,1)} reshape(bf16[32,2,24576]{2,1,0:T(2,128)(2,1)} %all-to-all-done.1) | data formatting | bytes 6291456
  393.0 8.7 %slice.64 = bf16[1,2784,512]{2,0,1:T(2,128)(2,1)} slice(bf16[1,3072,512]{2,0,1:T(2,128)(2,1)} %bitcast.53), slice={[0:1], [288:3072], [0:512]} | slice | bytes 5701632 | tf_op jit(solution)/shard_map/slice | solution.py:23
  401.7 0.0 slice-done
  401.7 6.3 %slice.63 = bf16[1,2880,512]{2,0,1:T(2,128)(2,1)S(1)} slice(bf16[1,3072,512]{2,0,1:T(2,128)(2,1)S(1)} %bitcast.56), slice={[0:1], [192:3072], [0:512]} | slice | bytes 5898240 | tf_op jit(solution)/shard_map/slice | solution.py:23
  408.0 6.5 %slice.62 = bf16[1,2976,512]{2,0,1:T(2,128)(2,1)S(1)} slice(bf16[1,3072,512]{2,0,1:T(2,128)(2,1)S(1)} %bitcast.57), slice={[0:1], [96:3072], [0:512]} | slice | bytes 6094848 | tf_op jit(solution)/shard_map/slice | solution.py:23
  414.5 0.8 copy.32
  415.3 3.4 copy.35
  418.7 0.9 copy.34
  419.6 0.9 copy.33
  420.5 4.4 %add_convert_fusion = bf16[32,96,512]{2,1,0:T(8,128)(2,1)} fusion(f32[32,96,512]{2,1,0:T(8,128)S(1)} %bitcast.59, bf16[29,96,512]{2,1,0:T(8,128)(2,1)S(1)} %bitcast.64, bf16[30,96,512]{2,1,0:T(8,128)(2,1)S(1)} %bitcast.63, bf16[31,96,512]{2,1,0:T(8,128)(2,1)S(1)} %bitcast.62, f32[32]{0:T(128)S(1)} %copy-done.6, f32[32]{0:T(128)S(1)} %copy-done.8, ...), kind=kLoop, calls=%fused_computation.9 | loop fusion | flops 17301504 | bytes 18285056 | tf_op jit(solution)/shard_map/convert_element_type | solution.py:75
  (27 shorter events, 0.1 us)
Async XLA Ops:
  7.2 314.4 %copy-start = (bf16[1,3072,512]{2,1,0:T(8,128)(2,1)S(1)}, bf16[1,3072,512]{2,1,0:T(8,128)(2,1)}, u32[]{:S(2)}) copy-start(bf16[1,3072,512]{2,1,0:T(8,128)(2,1)} %param.9) | copy-start | bytes 9437188
  7.2 3.9 copy-start.2
  11.1 4.0 copy-start.1
  16.7 0.6 copy-start.3
  16.7 0.6 copy-start.5
  16.7 0.6 copy-start.7
  16.7 0.6 copy-start.9
  24.8 49.8 %all-to-all-start = ((bf16[32,96,512]{2,1,0:T(8,128)(2,1)}), bf16[32,96,512]{2,1,0:T(8,128)(2,1)}, u32[]{:S(2)}, u32[]{:S(2)}) async-start(bf16[32,96,512]{2,1,0:T(8,128)(2,1)} %add_convert_fusion.1), calls=%async_computation | async-start | bytes 6291456 | tf_op jit(solution)/shard_map/all_to_all | solution.py:30
  74.6 5.5 %copy-start.11 = (s32[1,1,128]{2,1,0:T(1,128)S(1)}, s32[1,1,128]{2,1,0:T(1,128)}, u32[]{:S(2)}) copy-start(s32[1,1,128]{2,1,0:T(1,128)} %param.11) | copy-start | bytes 1540
  115.6 34.6 %copy-start.12 = (s32[1,1,128]{2,1,0:T(1,128)S(1)}, s32[1,1,128]{2,1,0:T(1,128)}, u32[]{:S(2)}) copy-start(s32[1,1,128]{2,1,0:T(1,128)} %param.12) | copy-start | bytes 1540
  316.5 57.6 %all-to-all-start.1 = ((bf16[32,2,24576]{2,1,0:T(2,128)(2,1)}), bf16[32,2,24576]{2,1,0:T(2,128)(2,1)}, u32[]{:S(2)}, u32[]{:S(2)}) async-start(bf16[32,2,24576]{2,1,0:T(2,128)(2,1)} %reshape.88), calls=%async_computation.1 | async-start | bytes 6291456 | tf_op jit(solution)/shard_map/all_to_all | solution.py:34
  321.3 50.5 %all-reduce.8.cloned.1.call-start = ((), (), s32[]{:S(2)}) async-start(), calls=%async_computation.2 | async-start | bytes 1048576 | tf_op jit(solution)/shard_map/psum | solution.py:65
  392.9 8.8 %slice-start = ((s8[6291456]{0:T(1024)(128)(4,1)}), s8[4194304]{0:T(1024)(128)(4,1)S(1)}, s32[]{:S(2)}) async-start(s8[6291456]{0:T(1024)(128)(4,1)} %bitcast.54), calls=%async_computation.3 | async-start | bytes 8388608
  393.0 8.8 %slice-start.1 = ((s8[6291456]{0:T(1024)(128)(4,1)}), s8[2097152]{0:T(1024)(128)(4,1)S(1)}, s32[]{:S(2)}) async-start(s8[6291456]{0:T(1024)(128)(4,1)} %bitcast.54), calls=%async_computation.4 | async-start | bytes 4194304
  419.6 0.9 copy-start.4
  419.6 0.9 copy-start.6
  419.6 0.9 copy-start.8
  419.6 0.9 copy-start.10
Sparse Core Ops, SparseCore 0:
  326.2 45.5 all-reduce.7
where the time goes:
time: 438 us; the launch traced here: 432 us
  local copies, waits for them, and re-layouts  167 us (38%)
  matrix products  116 us (26%)
  waiting for transfers between devices  86.8 us (20%)
  other arithmetic  33.9 us (8%)
  between operations  15.2 us (3%)
  starting transfers between devices  13.2 us (3%)
    dot_general x2, local copies, waits for them, and re-layouts, transposed_hop(): jnp.einsum('bij,bif->bjf', values, picked, preferred_element_type=jnp.flo...  69.2 us
    dot_general x2, matrix products, transposed_hop(): jnp.einsum('bij,bif->bjf', values, picked, preferred_element_type=jnp.flo...  46.7 us
    psum x1, waiting for transfers between devices, on_device(): lax.psum(terms.astype(jnp.bfloat16), 'cluster').astype(jnp.float32)  45.7 us
    all_to_all x1, waiting for transfers between devices, to_snapshots(): return lax.all_to_all(field, 'tm', split_axis=0, concat_axis=1, tiled=True)  41.1 us
    unnamed x38, local copies, waits for them, and re-layouts  36.6 us
    dot_general x2, matrix products, transposed_hop(): jnp.einsum('bk,bjf->kjf', cols_hot, prod, precision=lax.Precision.HIGHEST...  34.9 us
    convert_element_type x2, local copies, waits for them, and re-layouts, on_device(): transposed_hop(first, rows, cols, values, count).astype(jnp.bfloat16)[None]  30.4 us
    slice x6, local copies, waits for them, and re-layouts, local_band(): field[offset:]  29.2 us
  transfers between devices with their start and end apart: 3, of which 2 were waited for; matrix products, arithmetic and copies ran while one was open for 2% of the time, Pallas kernels for 0%

commit v1 on v0

v1 whole, which is shorter than its diff:
```python
import functools

import jax
import jax.numpy as jnp
from jax import lax
from jax.experimental import pallas as pl
from jax.experimental.pallas import tpu as pltpu
from jax.sharding import PartitionSpec as P

BAND = 4
BLK = 128
UNROLL = 16
bf16 = jnp.bfloat16
f32 = jnp.float32
VMEM_LIMIT = 56 * 2**20


def band_kernel(band_ref, field_ref, out_ref):
    total = field_ref.shape[0]
    widths = [band_ref[t] for t in range(total)]
    scales = [
        jnp.where(
            width == 1,
            f32(1.0),
            jnp.where(width == 2, f32(0.5), jnp.where(width == 3, f32(1.0 / 3.0), f32(0.25))),
        )
        for width in widths
    ]
    window = [field_ref[t].astype(f32) for t in range(BAND)]
    for s in range(total):
        result = scales[s] * window[0]
        for offset in range(1, BAND):
            if s + offset < total:
                factor = jnp.where(offset < widths[s + offset], scales[s + offset], f32(0.0))
                result = result + factor * window[offset]
        out_ref[s] = result.astype(out_ref.dtype)
        window = window[1:]
        if s + BAND < total:
            window.append(field_ref[s + BAND].astype(f32))


def band_apply(band, field, rows=16):
    total, verts, width = field.shape
    spec = pl.BlockSpec((total, rows, width), lambda i: (0, i, 0))
    return pl.pallas_call(
        band_kernel,
        grid=(verts // rows,),
        in_specs=[pl.BlockSpec(memory_space=pltpu.SMEM), spec],
        out_specs=spec,
        out_shape=jax.ShapeDtypeStruct(field.shape, bf16),
        compiler_params=pltpu.CompilerParams(vmem_limit_bytes=VMEM_LIMIT),
    )(band, field)


def prepare_kernel(
    rows_ref, cols_ref, count_ref, values_ref, weight_ref,
    tiles_ref, slot_rows_ref, slot_cols_ref, slots_ref, weight_t_ref, sizes, used,
):
    col_tiles = sizes.shape[0]
    slot_total = slot_cols_ref.shape[0]
    count = count_ref[0]
    tiles_ref[...] = jnp.zeros_like(tiles_ref)
    weight_t_ref[...] = weight_ref[...].T

    def clear(s, carry):
        slot_cols_ref[s] = 0
        slot_rows_ref[2 * s] = 0
        slot_rows_ref[2 * s + 1] = 0
        return carry

    lax.fori_loop(0, slot_total, clear, 0)
    for c in range(col_tiles):
        sizes[c] = 0

    def tally(b, carry):
        c = cols_ref[b]
        sizes[c] = sizes[c] + 1
        return carry

    lax.fori_loop(0, count, tally, 0)
    first = jnp.int32(0)
    for c in range(col_tiles):
        used[c] = 2 * first
        first = first + (sizes[c] + 1) // 2
    slots_ref[0] = first

    def place(b, carry):
        c = cols_ref[b]
        half = used[c]
        used[c] = half + 1
        slot_rows_ref[half] = rows_ref[b]
        slot_cols_ref[half // 2] = c
        tiles_ref[half] = values_ref[b].T
        return carry

    lax.fori_loop(0, count, place, 0)


def prepare(rows, cols, count, values, weight, col_tiles):
    blocks = values.shape[0]
    slot_total = -(-(blocks // 2 + col_tiles // 2) // UNROLL) * UNROLL
    smem = pl.BlockSpec(memory_space=pltpu.SMEM)
    vmem = pl.BlockSpec(memory_space=pltpu.VMEM)
    return pl.pallas_call(
        prepare_kernel,
        in_specs=[smem, smem, smem, vmem, vmem],
        out_specs=(vmem, smem, smem, smem, vmem),
        out_shape=(
            jax.ShapeDtypeStruct((2 * slot_total, BLK, BLK), bf16),
            jax.ShapeDtypeStruct((2 * slot_total,), jnp.int32),
            jax.ShapeDtypeStruct((slot_total,), jnp.int32),
            jax.ShapeDtypeStruct((1,), jnp.int32),
            jax.ShapeDtypeStruct(weight.shape, bf16),
        ),
        scratch_shapes=[
            pltpu.SMEM((col_tiles,), jnp.int32),
            pltpu.SMEM((col_tiles,), jnp.int32),
        ],
        compiler_params=pltpu.CompilerParams(vmem_limit_bytes=VMEM_LIMIT),
    )(rows, cols, count, values, weight)


def hops_kernel(
    slot_rows_ref, slot_cols_ref, slots_ref, dz_ref, weight_t_ref, tiles_ref, out_ref, feats, acc
):
    tiles = feats.shape[0]
    group = 4
    for t in range(0, tiles, group):
        pushed = jnp.dot(
            dz_ref[t * BLK : (t + group) * BLK, :], weight_t_ref[...], preferred_element_type=f32
        ).astype(bf16)
        for k in range(group):
            feats[t + k] = pushed[k * BLK : (k + 1) * BLK]

    def step(q, carry):
        for u in range(UNROLL):
            slot = q * UNROLL + u
            left = jnp.concatenate([tiles_ref[2 * slot], tiles_ref[2 * slot + 1]], axis=1)
            right = jnp.concatenate(
                [feats[slot_rows_ref[2 * slot]], feats[slot_rows_ref[2 * slot + 1]]], axis=0
            )
            c = slot_cols_ref[slot]
            acc[c] = acc[c] + jnp.dot(left, right, preferred_element_type=f32)
        return carry

    trips = (slots_ref[0] + UNROLL - 1) // UNROLL
    acc[...] = jnp.zeros_like(acc)
    lax.fori_loop(0, trips, step, 0)
    feats[...] = acc[...].astype(bf16)
    acc[...] = jnp.zeros_like(acc)
    lax.fori_loop(0, trips, step, 0)
    for t in range(tiles):
        out_ref[t * BLK : (t + 1) * BLK, :] = acc[t].astype(bf16)


def two_hops(slot_rows, slot_cols, slots, dz, weight_t, tiles):
    verts, width = dz.shape
    smem = pl.BlockSpec(memory_space=pltpu.SMEM)
    vmem = pl.BlockSpec(memory_space=pltpu.VMEM)
    return pl.pallas_call(
        hops_kernel,
        in_specs=[smem, smem, smem, vmem, vmem, vmem],
        out_specs=vmem,
        out_shape=jax.ShapeDtypeStruct((verts, width), bf16),
        scratch_shapes=[
            pltpu.VMEM((verts // BLK, BLK, width), bf16),
            pltpu.VMEM((verts // BLK, BLK, width), f32),
        ],
        compiler_params=pltpu.CompilerParams(vmem_limit_bytes=VMEM_LIMIT),
    )(slot_rows, slot_cols, slots, dz, weight_t, tiles)


def exchange(field):
    return lax.all_to_all(field, "tm", split_axis=0, concat_axis=0, tiled=True)


def cluster_sum(terms, n):
    me = lax.axis_index("cluster")
    parts = terms.astype(bf16).reshape(n, terms.shape[0] // n, terms.shape[1])

    def shift(array, k):
        return lax.ppermute(array, "cluster", [(i, (i + k) % n) for i in range(n)])

    def pick(stack, k):
        return lax.dynamic_index_in_dim(stack, k % n, 0, keepdims=False)

    total = pick(parts, me).astype(f32)
    for k in range(1, n):
        total = total + shift(pick(parts, me + k), k).astype(f32)
    share = total.astype(bf16)
    shares = jnp.stack([share] + [shift(share, k) for k in range(1, n)])
    whole = jnp.concatenate([pick(shares, me + n - q) for q in range(n)], axis=0)
    return whole.astype(f32)


def on_device(
    n_cluster, cotangent, propagated, weight, block_rows, block_cols, block_values, block_counts, band
):
    snaps, own, width = cotangent.shape
    verts = snaps * own
    dz = exchange(band_apply(band, cotangent)).reshape(verts, width)
    tiles, slot_rows, slot_cols, slots, weight_t = prepare(
        block_rows[0, 0], block_cols[0, 0], block_counts[0], block_values[0, 0], weight[0], verts // BLK
    )
    second = two_hops(slot_rows, slot_cols, slots, dz, weight_t, tiles)
    input_grad = band_apply(band, exchange(second.reshape(snaps, own, width)))
    terms = jnp.einsum("vf,vg->fg", propagated[0], dz, preferred_element_type=f32)
    weight_grad = cluster_sum(terms, n_cluster)
    return (input_grad, weight_grad[None])


def solution(mesh):
    placed = (
        P(None, ("cluster", "tm"), None),
        P("tm", "cluster", None),
        P("tm", None, None),
        P("tm", "cluster", None),
        P("tm", "cluster", None),
        P("tm", "cluster", None, None, None),
        P("tm", "cluster"),
        P(),
    )
    return jax.shard_map(
        functools.partial(on_device, mesh.shape["cluster"]),
        mesh=mesh,
        in_specs=placed,
        out_specs=(P(None, ("cluster", "tm"), None), P("tm", None, None)),
        check_vma=False,
    )
```

time: 438 us -> 123 us (0.28); the launches traced: 432 us -> 123 us
  local copies, waits for them, and re-layouts: 167 us -> 1.57 us
  matrix products: 116 us -> 3.72 us
  other arithmetic: 33.9 us -> 3.11 us
  Pallas kernels: 0 us -> 29.3 us
  waiting for transfers between devices: 86.8 us -> 59.9 us
  between operations: 15.2 us -> 1.4 us
  starting transfers between devices: 13.2 us -> 23.8 us
    dot_general x8 -> x1, matrix products: 116 us -> 3.72 us  [on_device(): jnp.einsum('vf,vg->fg', propagated[0], dz, preferred_element_type=f32)]
    dot_general x2 -> x0, local copies, waits for them, and re-layouts: 69.2 us -> none  [transposed_hop(): jnp.einsum('bij,bif->bjf', values, picked, preferred_element_type=jnp.flo...]
    psum x1 -> x0, waiting for transfers between devices: 45.7 us -> none  [on_device(): lax.psum(terms.astype(jnp.bfloat16), 'cluster').astype(jnp.float32)]
    unnamed x38 -> x4, local copies, waits for them, and re-layouts: 36.6 us -> 0.8 us
    convert_element_type x2 -> x0, local copies, waits for them, and re-layouts: 30.4 us -> none  [on_device(): transposed_hop(first, rows, cols, values, count).astype(jnp.bfloat16)[None]]
    slice x7 -> x0, local copies, waits for them, and re-layouts: 29.5 us -> none  [the longest x6 29.2 us: local_band(): field[offset:]]
    pallas_call x0 -> x4, Pallas kernels: none -> 29.3 us  [the longest x2 12 us: band_apply(): pl.pallas_call(band_kernel, grid=(verts // rows,), in_specs=[pl.BlockSpec...]
    unnamed x2 -> x0, other arithmetic: 21.9 us -> none
  transfers between devices with their start and end apart: 3 -> 8, of which waited for: 2 -> 8; matrix products, arithmetic and copies ran while one was open for 2% -> 6% of each run, Pallas kernels for 0% -> 6%
where the time goes in v1:
time: 123 us
  waiting for transfers between devices  59.9 us (49%)
  Pallas kernels  29.3 us (24%)
  starting transfers between devices  23.8 us (19%)
  matrix products  3.72 us (3%)
  other arithmetic  3.11 us (3%)
  local copies, waits for them, and re-layouts  1.57 us (1%)
  between operations  1.4 us (1%)
    all_to_all x2, waiting for transfers between devices, exchange(): return lax.all_to_all(field, 'tm', split_axis=0, concat_axis=0, tiled=True)  44.4 us
    all_to_all x2, starting transfers between devices, exchange(): return lax.all_to_all(field, 'tm', split_axis=0, concat_axis=0, tiled=True)  16 us
    ppermute x6, waiting for transfers between devices, shift(): return lax.ppermute(array, 'cluster', [(i, (i + k) % n) for i in range(n)])  15.4 us
    pallas_call x2, Pallas kernels, band_apply(): pl.pallas_call(band_kernel, grid=(verts // rows,), in_specs=[pl.BlockSpec...  12 us
    pallas_call x1, Pallas kernels, two_hops(): pl.pallas_call(hops_kernel, in_specs=[smem, smem, smem, vmem, vmem, vmem]...  10.4 us
    ppermute x6, starting transfers between devices, shift(): return lax.ppermute(array, 'cluster', [(i, (i + k) % n) for i in range(n)])  7.71 us
    pallas_call x1, Pallas kernels, prepare(): pl.pallas_call(prepare_kernel, in_specs=[smem, smem, smem, vmem, vmem], o...  6.78 us
    dot_general x1, matrix products, on_device(): jnp.einsum('vf,vg->fg', propagated[0], dz, preferred_element_type=f32)  3.72 us
  transfers between devices with their start and end apart: 8, of which 8 were waited for; matrix products, arithmetic and copies ran while one was open for 6% of the time, Pallas kernels for 6%

profile of v1, /device:TPU:0, one launch (start us, length us, event | category | flops | bytes accessed | tf_op | source)
XLA Modules:
  0.0 122.7 jit_solution(4865819536707182559)
XLA Ops:
  0.6 0.0 copy-start
  0.6 6.1 %shard_map.96 = bf16[32,96,512]{2,1,0:T(8,128)(2,1)} custom-call(s32[32]{0:T(128)} %band_ref.3, bf16[32,96,512]{2,1,0:T(8,128)(2,1)} %field_ref.1), custom_call_target="tpu_custom_call" | custom-call | tf_op jit(solution)/shard_map/pallas_call | solution.py:45
  6.7 7.5 %all-to-all-start = ((bf16[32,96,512]{2,1,0:T(8,128)(2,1)}), bf16[32,96,512]{2,1,0:T(8,128)(2,1)}, u32[]{:S(2)}, u32[]{:S(2)}) async-start(bf16[32,96,512]{2,1,0:T(8,128)(2,1)} %shard_map.96), calls=%async_computation | async-start | bytes 6291456 | tf_op jit(solution)/shard_map/all_to_all | solution.py:174
  14.9 6.8 %shard_map.95 = (bf16[160,128,128]{2,1,0:T(8,128)(2,1)}, s32[160]{0:T(256)}, s32[80]{0:T(128)}, s32[1]{0:T(128)}, bf16[512,512]{1,0:T(8,128)(2,1)}) custom-call(s32[128]{0:T(128)} %bitcast.38, s32[128]{0:T(128)} %bitcast.39, s32[1]{0:T(128)} %bitcast.29.count_ref, bf16[128,128,128]{2,1,0:T(8,128)(2,1)} %bitcast.31, bf16[512,512]{1,0:T(8,128)(2,1)} %bitcast.35), custom_call_target="tpu_custom_call" | custom-call | tf_op jit(solution)/shard_map/pallas_call | solution.py:104
  21.7 34.3 %all-to-all-done = bf16[32,96,512]{2,1,0:T(8,128)(2,1)} async-done(((bf16[32,96,512]{2,1,0:T(8,128)(2,1)}), bf16[32,96,512]{2,1,0:T(8,128)(2,1)}, u32[]{:S(2)}, u32[]{:S(2)}) %all-to-all-start) | async-done | bytes 3145760 | tf_op jit(solution)/shard_map/all_to_all | solution.py:174
  56.0 10.4 %shard_map.97 = bf16[3072,512]{1,0:T(8,128)(2,1)} custom-call(s32[160]{0:T(256)} %get-tuple-element.7.slot_rows_ref, s32[80]{0:T(128)} %get-tuple-element.8.slot_cols_ref, s32[1]{0:T(128)} %get-tuple-element.9.slots_ref, bf16[3072,512]{1,0:T(8,128)(2,1)} %bitcast.5.dz_ref, bf16[512,512]{1,0:T(8,128)(2,1)} %get-tuple-element.10.weight_t_ref, ...), custom_call_target="tpu_custom_call" | custom-call | tf_op jit(solution)/shard_map/pallas_call | solution.py:160
  66.5 8.5 %all-to-all-start.1 = ((bf16[32,96,512]{2,1,0:T(8,128)(2,1)}), bf16[32,96,512]{2,1,0:T(8,128)(2,1)}, u32[]{:S(2)}, u32[]{:S(2)}) async-start(bf16[32,96,512]{2,1,0:T(8,128)(2,1)} %bitcast.30), calls=%async_computation.1 | async-start | bytes 6291456 | tf_op jit(solution)/shard_map/all_to_all | solution.py:174
  75.1 0.0 copy-done
  75.1 3.7 %fusion.2 = bf16[512,512]{0,1:T(8,128)(2,1)S(1)} fusion(bf16[3072,512]{1,0:T(8,128)(2,1)} %bitcast.5.dz_ref, bf16[1,3072,512]{2,1,0:T(8,128)(2,1)S(1)} %copy-done), kind=kOutput, calls=%fused_computation.2 | convolution fusion | flops 1610874880 | bytes 6815744 | tf_op jit(solution)/shard_map/vf,vg->fg/dot_general | solution.py:207
  78.8 0.0 copy-start.1
  78.8 0.8 copy-done.1
  79.6 0.7 dynamic-slice_bitcast_fusion.2
  80.3 3.2 %collective-permute-start.2 = (bf16[128,512]{1,0:T(8,128)(2,1)}, bf16[128,512]{1,0:T(8,128)(2,1)S(1)}, u32[]{:S(2)}, u32[]{:S(2)}) collective-permute-start(bf16[128,512]{1,0:T(8,128)(2,1)} %get-tuple-element.17), channel_id=1, source_target_pairs={{0,3},{1,0},{2,1},{3,2},{4,7},{5,4},{6,5},{7,6},{8,11},{9,8},{10,9... | collective-permute-start | bytes 393224 | tf_op jit(solution)/shard_map/ppermute | solution.py:182
  83.5 0.7 collective-permute-start.1
  84.2 1.4 %collective-permute-start = (bf16[128,512]{1,0:T(8,128)(2,1)S(1)}, bf16[128,512]{1,0:T(8,128)(2,1)}, u32[]{:S(2)}, u32[]{:S(2)}) collective-permute-start(bf16[128,512]{1,0:T(8,128)(2,1)S(1)} %get-tuple-element.16), channel_id=1, source_target_pairs={{0,1},{1,2},{2,3},{3,0},{4,5},{5,6},{6,7},{7,4},{8,9},{9,10},{10,1... | collective-permute-start | bytes 393224 | tf_op jit(solution)/shard_map/ppermute | solution.py:182
  85.6 4.2 %collective-permute-done.2 = bf16[128,512]{1,0:T(8,128)(2,1)S(1)} collective-permute-done((bf16[128,512]{1,0:T(8,128)(2,1)}, bf16[128,512]{1,0:T(8,128)(2,1)S(1)}, u32[]{:S(2)}, u32[]{:S(2)}) %collective-permute-start.2) | collective-permute-done | bytes 131104 | tf_op jit(solution)/shard_map/ppermute | solution.py:182
  89.8 1.9 %collective-permute-done.1 = bf16[128,512]{1,0:T(8,128)(2,1)S(1)} collective-permute-done((bf16[128,512]{1,0:T(8,128)(2,1)}, bf16[128,512]{1,0:T(8,128)(2,1)S(1)}, u32[]{:S(2)}, u32[]{:S(2)}) %collective-permute-start.1) | collective-permute-done | bytes 131104 | tf_op jit(solution)/shard_map/ppermute | solution.py:182
  91.6 1.9 %collective-permute-done = bf16[128,512]{1,0:T(8,128)(2,1)} collective-permute-done((bf16[128,512]{1,0:T(8,128)(2,1)S(1)}, bf16[128,512]{1,0:T(8,128)(2,1)}, u32[]{:S(2)}, u32[]{:S(2)}) %collective-permute-start) | collective-permute-done | bytes 131104 | tf_op jit(solution)/shard_map/ppermute | solution.py:182
  93.5 1.0 fusion.7
  94.5 0.6 collective-permute-start.5
  95.2 0.9 collective-permute-start.4
  96.1 0.9 collective-permute-start.3
  96.9 4.0 %collective-permute-done.5 = bf16[128,512]{1,0:T(8,128)(2,1)S(1)} collective-permute-done((bf16[128,512]{1,0:T(8,128)(2,1)S(1)}, bf16[128,512]{1,0:T(8,128)(2,1)S(1)}, u32[]{:S(2)}, u32[]{:S(2)}) %collective-permute-start.5) | collective-permute-done | bytes 131104 | tf_op jit(solution)/shard_map/ppermute | solution.py:182
  100.9 1.6 %collective-permute-done.4 = bf16[128,512]{1,0:T(8,128)(2,1)S(1)} collective-permute-done((bf16[128,512]{1,0:T(8,128)(2,1)S(1)}, bf16[128,512]{1,0:T(8,128)(2,1)S(1)}, u32[]{:S(2)}, u32[]{:S(2)}) %collective-permute-start.4) | collective-permute-done | bytes 131104 | tf_op jit(solution)/shard_map/ppermute | solution.py:182
  102.6 1.9 %collective-permute-done.3 = bf16[128,512]{1,0:T(8,128)(2,1)} collective-permute-done((bf16[128,512]{1,0:T(8,128)(2,1)S(1)}, bf16[128,512]{1,0:T(8,128)(2,1)}, u32[]{:S(2)}, u32[]{:S(2)}) %collective-permute-start.3) | collective-permute-done | bytes 131104 | tf_op jit(solution)/shard_map/ppermute | solution.py:182
  104.5 1.0 pad_maximum_fusion
  105.5 1.1 maximum_convert_fusion
  106.6 10.1 %all-to-all-done.1.field_ref = bf16[32,96,512]{2,1,0:T(8,128)(2,1)} async-done(((bf16[32,96,512]{2,1,0:T(8,128)(2,1)}), bf16[32,96,512]{2,1,0:T(8,128)(2,1)}, u32[]{:S(2)}, u32[]{:S(2)}) %all-to-all-start.1) | async-done | bytes 3145760 | tf_op jit(solution)/shard_map/all_to_all | solution.py:174
  116.8 5.9 %shard_map.98 = bf16[32,96,512]{2,1,0:T(8,128)(2,1)} custom-call(s32[32]{0:T(128)} %band_ref.3, bf16[32,96,512]{2,1,0:T(8,128)(2,1)} %all-to-all-done.1.field_ref), custom_call_target="tpu_custom_call" | custom-call | tf_op jit(solution)/shard_map/pallas_call | solution.py:45
  (1 shorter events, 0.0 us)
Async XLA Ops:
  0.6 74.4 %copy-start = (bf16[1,3072,512]{2,1,0:T(8,128)(2,1)S(1)}, bf16[1,3072,512]{2,1,0:T(8,128)(2,1)}, u32[]{:S(2)}) copy-start(bf16[1,3072,512]{2,1,0:T(8,128)(2,1)} %param.9) | copy-start | bytes 9437188
  6.7 49.3 %all-to-all-start = ((bf16[32,96,512]{2,1,0:T(8,128)(2,1)}), bf16[32,96,512]{2,1,0:T(8,128)(2,1)}, u32[]{:S(2)}, u32[]{:S(2)}) async-start(bf16[32,96,512]{2,1,0:T(8,128)(2,1)} %shard_map.96), calls=%async_computation | async-start | bytes 6291456 | tf_op jit(solution)/shard_map/all_to_all | solution.py:174
  66.5 50.3 %all-to-all-start.1 = ((bf16[32,96,512]{2,1,0:T(8,128)(2,1)}), bf16[32,96,512]{2,1,0:T(8,128)(2,1)}, u32[]{:S(2)}, u32[]{:S(2)}) async-start(bf16[32,96,512]{2,1,0:T(8,128)(2,1)} %bitcast.30), calls=%async_computation.1 | async-start | bytes 6291456 | tf_op jit(solution)/shard_map/all_to_all | solution.py:174
  78.8 0.8 copy-start.1
  80.3 9.5 %collective-permute-start.2 = (bf16[128,512]{1,0:T(8,128)(2,1)}, bf16[128,512]{1,0:T(8,128)(2,1)S(1)}, u32[]{:S(2)}, u32[]{:S(2)}) collective-permute-start(bf16[128,512]{1,0:T(8,128)(2,1)} %get-tuple-element.17), channel_id=1, source_target_pairs={{0,3},{1,0},{2,1},{3,2},{4,7},{5,4},{6,5},{7,6},{8,11},{9,8},{10,9... | collective-permute-start | bytes 393224 | tf_op jit(solution)/shard_map/ppermute | solution.py:182
  83.5 8.1 %collective-permute-start.1 = (bf16[128,512]{1,0:T(8,128)(2,1)}, bf16[128,512]{1,0:T(8,128)(2,1)S(1)}, u32[]{:S(2)}, u32[]{:S(2)}) collective-permute-start(bf16[128,512]{1,0:T(8,128)(2,1)} %get-tuple-element.18), channel_id=1, source_target_pairs={{0,2},{1,3},{2,0},{3,1},{4,6},{5,7},{6,4},{7,5},{8,10},{9,11},{10,... | collective-permute-start | bytes 393224 | tf_op jit(solution)/shard_map/ppermute | solution.py:182
  84.2 9.3 %collective-permute-start = (bf16[128,512]{1,0:T(8,128)(2,1)S(1)}, bf16[128,512]{1,0:T(8,128)(2,1)}, u32[]{:S(2)}, u32[]{:S(2)}) collective-permute-start(bf16[128,512]{1,0:T(8,128)(2,1)S(1)} %get-tuple-element.16), channel_id=1, source_target_pairs={{0,1},{1,2},{2,3},{3,0},{4,5},{5,6},{6,7},{7,4},{8,9},{9,10},{10,1... | collective-permute-start | bytes 393224 | tf_op jit(solution)/shard_map/ppermute | solution.py:182
  94.5 6.4 %collective-permute-start.5 = (bf16[128,512]{1,0:T(8,128)(2,1)S(1)}, bf16[128,512]{1,0:T(8,128)(2,1)S(1)}, u32[]{:S(2)}, u32[]{:S(2)}) collective-permute-start(bf16[128,512]{1,0:T(8,128)(2,1)S(1)} %fusion.7), channel_id=1, source_target_pairs={{0,3},{1,0},{2,1},{3,2},{4,7},{5,4},{6,5},{7,6},{8,11},{9,8},{10,9... | collective-permute-start | bytes 393224 | tf_op jit(solution)/shard_map/ppermute | solution.py:182
  95.2 7.4 %collective-permute-start.4 = (bf16[128,512]{1,0:T(8,128)(2,1)S(1)}, bf16[128,512]{1,0:T(8,128)(2,1)S(1)}, u32[]{:S(2)}, u32[]{:S(2)}) collective-permute-start(bf16[128,512]{1,0:T(8,128)(2,1)S(1)} %fusion.7), channel_id=1, source_target_pairs={{0,2},{1,3},{2,0},{3,1},{4,6},{5,7},{6,4},{7,5},{8,10},{9,11},{10,... | collective-permute-start | bytes 393224 | tf_op jit(solution)/shard_map/ppermute | solution.py:182
  96.1 8.4 %collective-permute-start.3 = (bf16[128,512]{1,0:T(8,128)(2,1)S(1)}, bf16[128,512]{1,0:T(8,128)(2,1)}, u32[]{:S(2)}, u32[]{:S(2)}) collective-permute-start(bf16[128,512]{1,0:T(8,128)(2,1)S(1)} %fusion.7), channel_id=1, source_target_pairs={{0,1},{1,2},{2,3},{3,0},{4,5},{5,6},{6,7},{7,4},{8,9},{9,10},{10,1... | collective-permute-start | bytes 393224 | tf_op jit(solution)/shard_map/ppermute | solution.py:182

commit v2 on v1

--- a/solution.py
+++ b/solution.py
@@ -9,14 +9,27 @@
 
 BAND = 4
 BLK = 128
-UNROLL = 16
+UNROLL = 24
 bf16 = jnp.bfloat16
 f32 = jnp.float32
 VMEM_LIMIT = 56 * 2**20
 
 
-def band_kernel(band_ref, field_ref, out_ref):
-    total = field_ref.shape[0]
+def band_kernel(group, band_ref, field_hbm, out_hbm, field, out, in_sems, out_sems):
+    total, verts, width = field.shape
+    groups = total // group
+    rows, lanes = 16, 256
+
+    def pull(g):
+        part = pl.ds(g * group, group)
+        return pltpu.make_async_copy(field_hbm.at[part], field.at[part], in_sems.at[g])
+
+    def push(g):
+        part = pl.ds(g * group, group)
+        return pltpu.make_async_copy(out.at[part], out_hbm.at[part], out_sems.at[g])
+
+    for g in range(groups):
+        pull(g).start()
     widths = [band_ref[t] for t in range(total)]
     scales = [
         jnp.where(
@@ -26,28 +39,49 @@
         )
         for width in widths
     ]
-    window = [field_ref[t].astype(f32) for t in range(BAND)]
-    for s in range(total):
-        result = scales[s] * window[0]
-        for offset in range(1, BAND):
-            if s + offset < total:
-                factor = jnp.where(offset < widths[s + offset], scales[s + offset], f32(0.0))
-                result = result + factor * window[offset]
-        out_ref[s] = result.astype(out_ref.dtype)
-        window = window[1:]
-        if s + BAND < total:
-            window.append(field_ref[s + BAND].astype(f32))
-
-
-def band_apply(band, field, rows=16):
-    total, verts, width = field.shape
-    spec = pl.BlockSpec((total, rows, width), lambda i: (0, i, 0))
+    pull(0).wait()
+    for g in range(groups):
+        if g + 1 < groups:
+            pull(g + 1).wait()
+        start = g * group
+        stop = min(start + group + BAND - 1, total)
+        factors = [
+            [scales[s]]
+            + [
+                jnp.where(o < widths[s + o], scales[s + o], f32(0.0))
+                for o in range(1, BAND)
+                if s + o < total
+            ]
+            for s in range(start, start + group)
+        ]
+        for row in range(0, verts, rows):
+            for lane in range(0, width, lanes):
+                spot = (pl.ds(row, rows), pl.ds(lane, lanes))
+                window = [field[(t, *spot)].astype(f32) for t in range(start, stop)]
+                for k in range(group):
+                    result = factors[k][0] * window[k]
+                    for o in range(1, len(factors[k])):
+                        result = result + factors[k][o] * window[k + o]
+                    out[(start + k, *spot)] = result.astype(out.dtype)
+        push(g).start()
+    for g in range(groups):
+        push(g).wait()
+
+
+def band_apply(band, field, group=4):
+    total = field.shape[0]
+    hbm = pl.BlockSpec(memory_space=pltpu.HBM)
     return pl.pallas_call(
-        band_kernel,
-        grid=(verts // rows,),
-        in_specs=[pl.BlockSpec(memory_space=pltpu.SMEM), spec],
-        out_specs=spec,
+        functools.partial(band_kernel, group),
+        in_specs=[pl.BlockSpec(memory_space=pltpu.SMEM), hbm],
+        out_specs=hbm,
         out_shape=jax.ShapeDtypeStruct(field.shape, bf16),
+        scratch_shapes=[
+            pltpu.VMEM(field.shape, bf16),
+            pltpu.VMEM(field.shape, bf16),
+            pltpu.SemaphoreType.DMA((total // group,)),
+            pltpu.SemaphoreType.DMA((total // group,)),
+        ],
         compiler_params=pltpu.CompilerParams(vmem_limit_bytes=VMEM_LIMIT),
     )(band, field)
 
@@ -121,18 +155,47 @@
 
 
 def hops_kernel(
-    slot_rows_ref, slot_cols_ref, slots_ref, dz_ref, weight_t_ref, tiles_ref, out_ref, feats, acc
+    slot_rows_ref, slot_cols_ref, slots_ref, dz_hbm, weight_hbm, tiles_hbm, out_hbm,
+    dz, weight_t, tiles_ref, feats, first, second, weight_sem, dz_sems, tile_sems, out_sems,
 ):
     tiles = feats.shape[0]
-    group = 4
-    for t in range(0, tiles, group):
+    group = tiles // dz_sems.shape[0]
+    trips = (slots_ref[0] + UNROLL - 1) // UNROLL
+
+    def pull(k):
+        part = pl.ds(k * group * BLK, group * BLK)
+        return pltpu.make_async_copy(dz_hbm.at[part], dz.at[part], dz_sems.at[k])
+
+    def pull_tiles(q):
+        part = pl.ds(q * 2 * UNROLL, 2 * UNROLL)
+        return pltpu.make_async_copy(tiles_hbm.at[part], tiles_ref.at[part], tile_sems.at[q])
+
+    def push(c):
+        part = pl.ds(pl.multiple_of(c * BLK, BLK), BLK)
+        return pltpu.make_async_copy(dz.at[part], out_hbm.at[part], out_sems.at[c])
+
+    def start_tiles(q, carry):
+        pull_tiles(q).start()
+        return carry
+
+    pull_weight = pltpu.make_async_copy(weight_hbm, weight_t, weight_sem)
+    pull_weight.start()
+    for k in range(tiles // group):
+        pull(k).start()
+    first[...] = jnp.zeros_like(first)
+    second[...] = jnp.zeros_like(second)
+    pull_weight.wait()
+    for k in range(tiles // group):
+        pull(k).wait()
+        if k == tiles // group - 2:
+            lax.fori_loop(0, trips, start_tiles, 0)
         pushed = jnp.dot(
-            dz_ref[t * BLK : (t + group) * BLK, :], weight_t_ref[...], preferred_element_type=f32
+            dz[k * group * BLK : (k + 1) * group * BLK, :], weight_t[...], preferred_element_type=f32
         ).astype(bf16)
-        for k in range(group):
-            feats[t + k] = pushed[k * BLK : (k + 1) * BLK]
-
-    def step(q, carry):
+        for t in range(group):
+            feats[k * group + t] = pushed[t * BLK : (t + 1) * BLK]
+
+    def work(q, acc):
         for u in range(UNROLL):
             slot = q * UNROLL + u
             left = jnp.concatenate([tiles_ref[2 * slot], tiles_ref[2 * slot + 1]], axis=1)
@@ -141,30 +204,54 @@
             )
             c = slot_cols_ref[slot]
             acc[c] = acc[c] + jnp.dot(left, right, preferred_element_type=f32)
-        return carry
-
-    trips = (slots_ref[0] + UNROLL - 1) // UNROLL
-    acc[...] = jnp.zeros_like(acc)
-    lax.fori_loop(0, trips, step, 0)
-    feats[...] = acc[...].astype(bf16)
-    acc[...] = jnp.zeros_like(acc)
-    lax.fori_loop(0, trips, step, 0)
-    for t in range(tiles):
-        out_ref[t * BLK : (t + 1) * BLK, :] = acc[t].astype(bf16)
+
+    def first_hop(q, carry):
+        pull_tiles(q).wait()
+        work(q, first)
+        return carry
+
+    def second_hop(q, done):
+        work(q, second)
+        ahead = jnp.minimum((q + 1) * UNROLL, slot_cols_ref.shape[0] - 1)
+        upto = jnp.where(q + 1 < trips, slot_cols_ref[ahead], tiles)
+
+        def finish(c, carry):
+            dz[pl.ds(pl.multiple_of(c * BLK, BLK), BLK), :] = second[c].astype(bf16)
+            push(c).start()
+            return carry
+
+        lax.fori_loop(done, upto, finish, 0)
+        return upto
+
+    lax.fori_loop(0, trips, first_hop, 0)
+    feats[...] = first[...].astype(bf16)
+    lax.fori_loop(0, trips, second_hop, jnp.int32(0))
+    for c in range(tiles):
+        push(c).wait()
 
 
 def two_hops(slot_rows, slot_cols, slots, dz, weight_t, tiles):
     verts, width = dz.shape
+    col_tiles = verts // BLK
+    parts = 4
     smem = pl.BlockSpec(memory_space=pltpu.SMEM)
-    vmem = pl.BlockSpec(memory_space=pltpu.VMEM)
+    hbm = pl.BlockSpec(memory_space=pltpu.HBM)
     return pl.pallas_call(
         hops_kernel,
-        in_specs=[smem, smem, smem, vmem, vmem, vmem],
-        out_specs=vmem,
+        in_specs=[smem, smem, smem, hbm, hbm, hbm],
+        out_specs=hbm,
         out_shape=jax.ShapeDtypeStruct((verts, width), bf16),
         scratch_shapes=[
-            pltpu.VMEM((verts // BLK, BLK, width), bf16),
-            pltpu.VMEM((verts // BLK, BLK, width), f32),
+            pltpu.VMEM((verts, width), bf16),
+            pltpu.VMEM(weight_t.shape, bf16),
+            pltpu.VMEM(tiles.shape, bf16),
+            pltpu.VMEM((col_tiles, BLK, width), bf16),
+            pltpu.VMEM((col_tiles, BLK, width), f32),
+            pltpu.VMEM((col_tiles, BLK, width), f32),
+            pltpu.SemaphoreType.DMA,
+            pltpu.SemaphoreType.DMA((parts,)),
+            pltpu.SemaphoreType.DMA((tiles.shape[0] // (2 * UNROLL),)),
+            pltpu.SemaphoreType.DMA((col_tiles,)),
         ],
         compiler_params=pltpu.CompilerParams(vmem_limit_bytes=VMEM_LIMIT),
     )(slot_rows, slot_cols, slots, dz, weight_t, tiles)

time: 123 us -> 119 us (0.967); the launches traced: 123 us -> 117 us
  starting transfers between devices: 23.8 us -> 21.6 us
  Pallas kernels: 29.3 us -> 27.3 us
  waiting for transfers between devices: 59.9 us -> 58.3 us
    pallas_call x3, Pallas kernels: 22.5 us -> 19.1 us  [the longest x1 9.81 us: two_hops(): pl.pallas_call(hops_kernel, in_specs=[smem, smem, smem, hbm, hbm, hbm], o...]
    all_to_all x2, starting transfers between devices: 16 us -> 13.8 us  [exchange(): return lax.all_to_all(field, 'tm', split_axis=0, concat_axis=0, tiled=True)]
    all_to_all x2, waiting for transfers between devices: 44.4 us -> 42.6 us  [exchange(): return lax.all_to_all(field, 'tm', split_axis=0, concat_axis=0, tiled=True)]
    pallas_call x1, Pallas kernels: 6.78 us -> 8.23 us  [prepare(): pl.pallas_call(prepare_kernel, in_specs=[smem, smem, smem, vmem, vmem], o...]
  transfers between devices with their start and end apart: 8 -> 8, of which waited for: 8 -> 8; matrix products, arithmetic and copies ran while one was open for 6% -> 6% of each run, Pallas kernels for 6% -> 7%
where the time goes in v2:
time: 119 us; the launch traced here: 117 us
  waiting for transfers between devices  58.3 us (49%)
  Pallas kernels  27.3 us (23%)
  starting transfers between devices  21.6 us (18%)
  matrix products  3.72 us (3%)
  other arithmetic  3.11 us (3%)
  local copies, waits for them, and re-layouts  1.57 us (1%)
  between operations  1.57 us (1%)
    all_to_all x2, waiting for transfers between devices, exchange(): return lax.all_to_all(field, 'tm', split_axis=0, concat_axis=0, tiled=True)  42.6 us
    ppermute x6, waiting for transfers between devices, shift(): return lax.ppermute(array, 'cluster', [(i, (i + k) % n) for i in range(n)])  15.7 us
    all_to_all x2, starting transfers between devices, exchange(): return lax.all_to_all(field, 'tm', split_axis=0, concat_axis=0, tiled=True)  13.8 us
    pallas_call x1, Pallas kernels, two_hops(): pl.pallas_call(hops_kernel, in_specs=[smem, smem, smem, hbm, hbm, hbm], o...  9.81 us
    pallas_call x2, Pallas kernels, band_apply(): pl.pallas_call(functools.partial(band_kernel, group), in_specs=[pl.BlockS...  9.25 us
    pallas_call x1, Pallas kernels, prepare(): pl.pallas_call(prepare_kernel, in_specs=[smem, smem, smem, vmem, vmem], o...  8.23 us
    ppermute x6, starting transfers between devices, shift(): return lax.ppermute(array, 'cluster', [(i, (i + k) % n) for i in range(n)])  7.82 us
    dot_general x1, matrix products, on_device(): jnp.einsum('vf,vg->fg', propagated[0], dz, preferred_element_type=f32)  3.72 us
  transfers between devices with their start and end apart: 8, of which 8 were waited for; matrix products, arithmetic and copies ran while one was open for 6% of the time, Pallas kernels for 7%

profile of v2, /device:TPU:0, one launch (start us, length us, event | category | flops | bytes accessed | tf_op | source)
XLA Modules:
  0.0 117.2 jit_solution(14271600889678429603)
XLA Ops:
  0.6 0.0 copy-start
  0.6 4.8 %shard_map.96 = bf16[32,96,512]{2,1,0:T(8,128)(2,1)} custom-call(s32[32]{0:T(128)} %band_ref.3, bf16[32,96,512]{2,1,0:T(8,128)(2,1)} %field_hbm.1), custom_call_target="tpu_custom_call" | custom-call | tf_op jit(solution)/shard_map/pallas_call | solution.py:74
  5.4 7.5 %all-to-all-start = ((bf16[32,96,512]{2,1,0:T(8,128)(2,1)}), bf16[32,96,512]{2,1,0:T(8,128)(2,1)}, u32[]{:S(2)}, u32[]{:S(2)}) async-start(bf16[32,96,512]{2,1,0:T(8,128)(2,1)} %shard_map.96), calls=%async_computation | async-start | bytes 6291456 | tf_op jit(solution)/shard_map/all_to_all | solution.py:261
  13.6 8.2 %shard_map.95 = (bf16[192,128,128]{2,1,0:T(8,128)(2,1)}, s32[192]{0:T(256)}, s32[96]{0:T(128)}, s32[1]{0:T(128)}, bf16[512,512]{1,0:T(8,128)(2,1)}) custom-call(s32[128]{0:T(128)} %bitcast.38, s32[128]{0:T(128)} %bitcast.39, s32[1]{0:T(128)} %bitcast.29.count_ref, bf16[128,128,128]{2,1,0:T(8,128)(2,1)} %bitcast.31, bf16[512,512]{1,0:T(8,128)(2,1)} %bitcast.35), custom_call_target="tpu_custom_call" | custom-call | tf_op jit(solution)/shard_map/pallas_call | solution.py:138
  21.8 32.9 %all-to-all-done = bf16[32,96,512]{2,1,0:T(8,128)(2,1)} async-done(((bf16[32,96,512]{2,1,0:T(8,128)(2,1)}), bf16[32,96,512]{2,1,0:T(8,128)(2,1)}, u32[]{:S(2)}, u32[]{:S(2)}) %all-to-all-start) | async-done | bytes 3145760 | tf_op jit(solution)/shard_map/all_to_all | solution.py:261
  54.7 9.8 %shard_map.97 = bf16[3072,512]{1,0:T(8,128)(2,1)} custom-call(s32[192]{0:T(256)} %get-tuple-element.7.slot_rows_ref, s32[96]{0:T(128)} %get-tuple-element.8.slot_cols_ref, s32[1]{0:T(128)} %get-tuple-element.9.slots_ref, bf16[3072,512]{1,0:T(8,128)(2,1)} %bitcast.5.dz_hbm, bf16[512,512]{1,0:T(8,128)(2,1)} %get-tuple-element.10.weight_hbm, ...), custom_call_target="tpu_custom_call" | custom-call | tf_op jit(solution)/shard_map/pallas_call | solution.py:239
  64.5 6.3 %all-to-all-start.1 = ((bf16[32,96,512]{2,1,0:T(8,128)(2,1)}), bf16[32,96,512]{2,1,0:T(8,128)(2,1)}, u32[]{:S(2)}, u32[]{:S(2)}) async-start(bf16[32,96,512]{2,1,0:T(8,128)(2,1)} %bitcast.30), calls=%async_computation.1 | async-start | bytes 6291456 | tf_op jit(solution)/shard_map/all_to_all | solution.py:261
  70.8 0.0 copy-done
  70.8 3.7 %fusion.2 = bf16[512,512]{0,1:T(8,128)(2,1)S(1)} fusion(bf16[3072,512]{1,0:T(8,128)(2,1)} %bitcast.5.dz_hbm, bf16[1,3072,512]{2,1,0:T(8,128)(2,1)S(1)} %copy-done), kind=kOutput, calls=%fused_computation.2 | convolution fusion | flops 1610874880 | bytes 6815744 | tf_op jit(solution)/shard_map/vf,vg->fg/dot_general | solution.py:294
  74.6 0.0 copy-start.1
  74.6 0.8 copy-done.1
  75.4 0.7 dynamic-slice_bitcast_fusion.2
  76.1 4.1 %collective-permute-start.2 = (bf16[128,512]{1,0:T(8,128)(2,1)}, bf16[128,512]{1,0:T(8,128)(2,1)S(1)}, u32[]{:S(2)}, u32[]{:S(2)}) collective-permute-start(bf16[128,512]{1,0:T(8,128)(2,1)} %get-tuple-element.17), channel_id=1, source_target_pairs={{0,3},{1,0},{2,1},{3,2},{4,7},{5,4},{6,5},{7,6},{8,11},{9,8},{10,9... | collective-permute-start | bytes 393224 | tf_op jit(solution)/shard_map/ppermute | solution.py:269
  80.2 0.0 collective-permute-start.1
  80.2 1.3 %collective-permute-start = (bf16[128,512]{1,0:T(8,128)(2,1)S(1)}, bf16[128,512]{1,0:T(8,128)(2,1)}, u32[]{:S(2)}, u32[]{:S(2)}) collective-permute-start(bf16[128,512]{1,0:T(8,128)(2,1)S(1)} %get-tuple-element.16), channel_id=1, source_target_pairs={{0,1},{1,2},{2,3},{3,0},{4,5},{5,6},{6,7},{7,4},{8,9},{9,10},{10,1... | collective-permute-start | bytes 393224 | tf_op jit(solution)/shard_map/ppermute | solution.py:269
  81.5 5.0 %collective-permute-done.2 = bf16[128,512]{1,0:T(8,128)(2,1)S(1)} collective-permute-done((bf16[128,512]{1,0:T(8,128)(2,1)}, bf16[128,512]{1,0:T(8,128)(2,1)S(1)}, u32[]{:S(2)}, u32[]{:S(2)}) %collective-permute-start.2) | collective-permute-done | bytes 131104 | tf_op jit(solution)/shard_map/ppermute | solution.py:269
  86.4 1.8 %collective-permute-done.1 = bf16[128,512]{1,0:T(8,128)(2,1)S(1)} collective-permute-done((bf16[128,512]{1,0:T(8,128)(2,1)}, bf16[128,512]{1,0:T(8,128)(2,1)S(1)}, u32[]{:S(2)}, u32[]{:S(2)}) %collective-permute-start.1) | collective-permute-done | bytes 131104 | tf_op jit(solution)/shard_map/ppermute | solution.py:269
  88.3 1.4 %collective-permute-done = bf16[128,512]{1,0:T(8,128)(2,1)} collective-permute-done((bf16[128,512]{1,0:T(8,128)(2,1)S(1)}, bf16[128,512]{1,0:T(8,128)(2,1)}, u32[]{:S(2)}, u32[]{:S(2)}) %collective-permute-start) | collective-permute-done | bytes 131104 | tf_op jit(solution)/shard_map/ppermute | solution.py:269
  89.6 1.0 fusion.7
  90.7 1.4 %collective-permute-start.5 = (bf16[128,512]{1,0:T(8,128)(2,1)S(1)}, bf16[128,512]{1,0:T(8,128)(2,1)S(1)}, u32[]{:S(2)}, u32[]{:S(2)}) collective-permute-start(bf16[128,512]{1,0:T(8,128)(2,1)S(1)} %fusion.7), channel_id=1, source_target_pairs={{0,3},{1,0},{2,1},{3,2},{4,7},{5,4},{6,5},{7,6},{8,11},{9,8},{10,9... | collective-permute-start | bytes 393224 | tf_op jit(solution)/shard_map/ppermute | solution.py:269
  92.0 0.2 collective-permute-start.4
  92.3 0.9 collective-permute-start.3
  93.1 4.1 %collective-permute-done.5 = bf16[128,512]{1,0:T(8,128)(2,1)S(1)} collective-permute-done((bf16[128,512]{1,0:T(8,128)(2,1)S(1)}, bf16[128,512]{1,0:T(8,128)(2,1)S(1)}, u32[]{:S(2)}, u32[]{:S(2)}) %collective-permute-start.5) | collective-permute-done | bytes 131104 | tf_op jit(solution)/shard_map/ppermute | solution.py:269
  97.2 2.2 %collective-permute-done.4 = bf16[128,512]{1,0:T(8,128)(2,1)S(1)} collective-permute-done((bf16[128,512]{1,0:T(8,128)(2,1)S(1)}, bf16[128,512]{1,0:T(8,128)(2,1)S(1)}, u32[]{:S(2)}, u32[]{:S(2)}) %collective-permute-start.4) | collective-permute-done | bytes 131104 | tf_op jit(solution)/shard_map/ppermute | solution.py:269
  99.5 1.2 %collective-permute-done.3 = bf16[128,512]{1,0:T(8,128)(2,1)} collective-permute-done((bf16[128,512]{1,0:T(8,128)(2,1)S(1)}, bf16[128,512]{1,0:T(8,128)(2,1)}, u32[]{:S(2)}, u32[]{:S(2)}) %collective-permute-start.3) | collective-permute-done | bytes 131104 | tf_op jit(solution)/shard_map/ppermute | solution.py:269
  100.7 1.0 pad_maximum_fusion
  101.7 1.1 maximum_convert_fusion
  102.8 9.7 %all-to-all-done.1.field_hbm = bf16[32,96,512]{2,1,0:T(8,128)(2,1)} async-done(((bf16[32,96,512]{2,1,0:T(8,128)(2,1)}), bf16[32,96,512]{2,1,0:T(8,128)(2,1)}, u32[]{:S(2)}, u32[]{:S(2)}) %all-to-all-start.1) | async-done | bytes 3145760 | tf_op jit(solution)/shard_map/all_to_all | solution.py:261
  112.6 4.5 %shard_map.98 = bf16[32,96,512]{2,1,0:T(8,128)(2,1)} custom-call(s32[32]{0:T(128)} %band_ref.3, bf16[32,96,512]{2,1,0:T(8,128)(2,1)} %all-to-all-done.1.field_hbm), custom_call_target="tpu_custom_call" | custom-call | tf_op jit(solution)/shard_map/pallas_call | solution.py:74
  (1 shorter events, 0.0 us)
Async XLA Ops:
  0.6 70.2 %copy-start = (bf16[1,3072,512]{2,1,0:T(8,128)(2,1)S(1)}, bf16[1,3072,512]{2,1,0:T(8,128)(2,1)}, u32[]{:S(2)}) copy-start(bf16[1,3072,512]{2,1,0:T(8,128)(2,1)} %param.9) | copy-start | bytes 9437188
  5.4 49.3 %all-to-all-start = ((bf16[32,96,512]{2,1,0:T(8,128)(2,1)}), bf16[32,96,512]{2,1,0:T(8,128)(2,1)}, u32[]{:S(2)}, u32[]{:S(2)}) async-start(bf16[32,96,512]{2,1,0:T(8,128)(2,1)} %shard_map.96), calls=%async_computation | async-start | bytes 6291456 | tf_op jit(solution)/shard_map/all_to_all | solution.py:261
  64.5 48.0 %all-to-all-start.1 = ((bf16[32,96,512]{2,1,0:T(8,128)(2,1)}), bf16[32,96,512]{2,1,0:T(8,128)(2,1)}, u32[]{:S(2)}, u32[]{:S(2)}) async-start(bf16[32,96,512]{2,1,0:T(8,128)(2,1)} %bitcast.30), calls=%async_computation.1 | async-start | bytes 6291456 | tf_op jit(solution)/shard_map/all_to_all | solution.py:261
  74.6 0.8 copy-start.1
  76.1 10.3 %collective-permute-start.2 = (bf16[128,512]{1,0:T(8,128)(2,1)}, bf16[128,512]{1,0:T(8,128)(2,1)S(1)}, u32[]{:S(2)}, u32[]{:S(2)}) collective-permute-start(bf16[128,512]{1,0:T(8,128)(2,1)} %get-tuple-element.17), channel_id=1, source_target_pairs={{0,3},{1,0},{2,1},{3,2},{4,7},{5,4},{6,5},{7,6},{8,11},{9,8},{10,9... | collective-permute-start | bytes 393224 | tf_op jit(solution)/shard_map/ppermute | solution.py:269
  80.2 8.1 %collective-permute-start.1 = (bf16[128,512]{1,0:T(8,128)(2,1)}, bf16[128,512]{1,0:T(8,128)(2,1)S(1)}, u32[]{:S(2)}, u32[]{:S(2)}) collective-permute-start(bf16[128,512]{1,0:T(8,128)(2,1)} %get-tuple-element.18), channel_id=1, source_target_pairs={{0,2},{1,3},{2,0},{3,1},{4,6},{5,7},{6,4},{7,5},{8,10},{9,11},{10,... | collective-permute-start | bytes 393224 | tf_op jit(solution)/shard_map/ppermute | solution.py:269
  80.2 9.5 %collective-permute-start = (bf16[128,512]{1,0:T(8,128)(2,1)S(1)}, bf16[128,512]{1,0:T(8,128)(2,1)}, u32[]{:S(2)}, u32[]{:S(2)}) collective-permute-start(bf16[128,512]{1,0:T(8,128)(2,1)S(1)} %get-tuple-element.16), channel_id=1, source_target_pairs={{0,1},{1,2},{2,3},{3,0},{4,5},{5,6},{6,7},{7,4},{8,9},{9,10},{10,1... | collective-permute-start | bytes 393224 | tf_op jit(solution)/shard_map/ppermute | solution.py:269
  90.7 6.6 %collective-permute-start.5 = (bf16[128,512]{1,0:T(8,128)(2,1)S(1)}, bf16[128,512]{1,0:T(8,128)(2,1)S(1)}, u32[]{:S(2)}, u32[]{:S(2)}) collective-permute-start(bf16[128,512]{1,0:T(8,128)(2,1)S(1)} %fusion.7), channel_id=1, source_target_pairs={{0,3},{1,0},{2,1},{3,2},{4,7},{5,4},{6,5},{7,6},{8,11},{9,8},{10,9... | collective-permute-start | bytes 393224 | tf_op jit(solution)/shard_map/ppermute | solution.py:269
  92.0 7.4 %collective-permute-start.4 = (bf16[128,512]{1,0:T(8,128)(2,1)S(1)}, bf16[128,512]{1,0:T(8,128)(2,1)S(1)}, u32[]{:S(2)}, u32[]{:S(2)}) collective-permute-start(bf16[128,512]{1,0:T(8,128)(2,1)S(1)} %fusion.7), channel_id=1, source_target_pairs={{0,2},{1,3},{2,0},{3,1},{4,6},{5,7},{6,4},{7,5},{8,10},{9,11},{10,... | collective-permute-start | bytes 393224 | tf_op jit(solution)/shard_map/ppermute | solution.py:269
  92.3 8.4 %collective-permute-start.3 = (bf16[128,512]{1,0:T(8,128)(2,1)S(1)}, bf16[128,512]{1,0:T(8,128)(2,1)}, u32[]{:S(2)}, u32[]{:S(2)}) collective-permute-start(bf16[128,512]{1,0:T(8,128)(2,1)S(1)} %fusion.7), channel_id=1, source_target_pairs={{0,1},{1,2},{2,3},{3,0},{4,5},{5,6},{6,7},{7,4},{8,9},{9,10},{10,1... | collective-permute-start | bytes 393224 | tf_op jit(solution)/shard_map/ppermute | solution.py:269

commit v3 on v2

--- a/solution.py
+++ b/solution.py
@@ -9,7 +9,8 @@
 
 BAND = 4
 BLK = 128
-UNROLL = 24
+SHORT = 8
+LONG = 24
 bf16 = jnp.bfloat16
 f32 = jnp.float32
 VMEM_LIMIT = 56 * 2**20
@@ -132,7 +133,7 @@
 
 def prepare(rows, cols, count, values, weight, col_tiles):
     blocks = values.shape[0]
-    slot_total = -(-(blocks // 2 + col_tiles // 2) // UNROLL) * UNROLL
+    slot_total = -(-(blocks // 2 + col_tiles // 2) // SHORT) * SHORT
     smem = pl.BlockSpec(memory_space=pltpu.SMEM)
     vmem = pl.BlockSpec(memory_space=pltpu.VMEM)
     return pl.pallas_call(
@@ -160,14 +161,15 @@
 ):
     tiles = feats.shape[0]
     group = tiles // dz_sems.shape[0]
-    trips = (slots_ref[0] + UNROLL - 1) // UNROLL
+    units = (slots_ref[0] + SHORT - 1) // SHORT
+    trips = units // (LONG // SHORT)
 
     def pull(k):
         part = pl.ds(k * group * BLK, group * BLK)
         return pltpu.make_async_copy(dz_hbm.at[part], dz.at[part], dz_sems.at[k])
 
     def pull_tiles(q):
-        part = pl.ds(q * 2 * UNROLL, 2 * UNROLL)
+        part = pl.ds(q * 2 * SHORT, 2 * SHORT)
         return pltpu.make_async_copy(tiles_hbm.at[part], tiles_ref.at[part], tile_sems.at[q])
 
     def push(c):
@@ -187,17 +189,17 @@
     pull_weight.wait()
     for k in range(tiles // group):
         pull(k).wait()
-        if k == tiles // group - 2:
-            lax.fori_loop(0, trips, start_tiles, 0)
+        if k == 0:
+            lax.fori_loop(0, units, start_tiles, 0)
         pushed = jnp.dot(
             dz[k * group * BLK : (k + 1) * group * BLK, :], weight_t[...], preferred_element_type=f32
         ).astype(bf16)
         for t in range(group):
             feats[k * group + t] = pushed[t * BLK : (t + 1) * BLK]
 
-    def work(q, acc):
-        for u in range(UNROLL):
-            slot = q * UNROLL + u
+    def work(start, length, acc):
+        for u in range(length):
+            slot = start + u
             left = jnp.concatenate([tiles_ref[2 * slot], tiles_ref[2 * slot + 1]], axis=1)
             right = jnp.concatenate(
                 [feats[slot_rows_ref[2 * slot]], feats[slot_rows_ref[2 * slot + 1]]], axis=0
@@ -205,27 +207,34 @@
             c = slot_cols_ref[slot]
             acc[c] = acc[c] + jnp.dot(left, right, preferred_element_type=f32)
 
-    def first_hop(q, carry):
-        pull_tiles(q).wait()
-        work(q, first)
-        return carry
-
-    def second_hop(q, done):
-        work(q, second)
-        ahead = jnp.minimum((q + 1) * UNROLL, slot_cols_ref.shape[0] - 1)
-        upto = jnp.where(q + 1 < trips, slot_cols_ref[ahead], tiles)
-
-        def finish(c, carry):
-            dz[pl.ds(pl.multiple_of(c * BLK, BLK), BLK), :] = second[c].astype(bf16)
-            push(c).start()
-            return carry
-
+    def finish(c, carry):
+        dz[pl.ds(pl.multiple_of(c * BLK, BLK), BLK), :] = second[c].astype(bf16)
+        push(c).start()
+        return carry
+
+    def first_hop(length, q, carry):
+        for k in range(length // SHORT):
+            pull_tiles(q * (length // SHORT) + k).wait()
+        work(q * length, length, first)
+        return carry
+
+    def second_hop(length, q, done):
+        work(q * length, length, second)
+        after = (q + 1) * length
+        upto = jnp.where(
+            after < units * SHORT,
+            slot_cols_ref[jnp.minimum(after, slot_cols_ref.shape[0] - 1)],
+            tiles,
+        )
         lax.fori_loop(done, upto, finish, 0)
         return upto
 
-    lax.fori_loop(0, trips, first_hop, 0)
+    rest = trips * (LONG // SHORT)
+    lax.fori_loop(0, trips, functools.partial(first_hop, LONG), 0)
+    lax.fori_loop(rest, units, functools.partial(first_hop, SHORT), 0)
     feats[...] = first[...].astype(bf16)
-    lax.fori_loop(0, trips, second_hop, jnp.int32(0))
+    done = lax.fori_loop(0, trips, functools.partial(second_hop, LONG), jnp.int32(0))
+    lax.fori_loop(rest, units, functools.partial(second_hop, SHORT), done)
     for c in range(tiles):
         push(c).wait()
 
@@ -233,7 +242,7 @@
 def two_hops(slot_rows, slot_cols, slots, dz, weight_t, tiles):
     verts, width = dz.shape
     col_tiles = verts // BLK
-    parts = 4
+    parts = 2
     smem = pl.BlockSpec(memory_space=pltpu.SMEM)
     hbm = pl.BlockSpec(memory_space=pltpu.HBM)
     return pl.pallas_call(
@@ -250,7 +259,7 @@
             pltpu.VMEM((col_tiles, BLK, width), f32),
             pltpu.SemaphoreType.DMA,
             pltpu.SemaphoreType.DMA((parts,)),
-            pltpu.SemaphoreType.DMA((tiles.shape[0] // (2 * UNROLL),)),
+            pltpu.SemaphoreType.DMA((tiles.shape[0] // (2 * SHORT),)),
             pltpu.SemaphoreType.DMA((col_tiles,)),
         ],
         compiler_params=pltpu.CompilerParams(vmem_limit_bytes=VMEM_LIMIT),

time: 119 us -> 117 us (0.983); the launches traced: 117 us -> 117 us
  Pallas kernels: 27.3 us -> 23.9 us
  waiting for transfers between devices: 58.3 us -> 60.5 us
    pallas_call x1, Pallas kernels: 9.81 us -> 7.96 us  [two_hops(): pl.pallas_call(hops_kernel, in_specs=[smem, smem, smem, hbm, hbm, hbm], o...]
    all_to_all x2, waiting for transfers between devices: 42.6 us -> 44.3 us  [exchange(): return lax.all_to_all(field, 'tm', split_axis=0, concat_axis=0, tiled=True)]
    pallas_call x1, Pallas kernels: 8.23 us -> 6.7 us  [prepare(): pl.pallas_call(prepare_kernel, in_specs=[smem, smem, smem, vmem, vmem], o...]
    all_to_all x2, starting transfers between devices: 13.8 us -> 15 us  [exchange(): return lax.all_to_all(field, 'tm', split_axis=0, concat_axis=0, tiled=True)]
  transfers between devices with their start and end apart: 8 -> 8, of which waited for: 8 -> 8; matrix products, arithmetic and copies ran while one was open for 6% -> 7% of each run, Pallas kernels for 7% -> 6%
where the time goes in v3:
time: 117 us
  waiting for transfers between devices  60.5 us (52%)
  Pallas kernels  23.9 us (20%)
  starting transfers between devices  22.2 us (19%)
  matrix products  3.72 us (3%)
  other arithmetic  3.11 us (3%)
  local copies, waits for them, and re-layouts  1.57 us (1%)
  between operations  1.57 us (1%)
    all_to_all x2, waiting for transfers between devices, exchange(): return lax.all_to_all(field, 'tm', split_axis=0, concat_axis=0, tiled=True)  44.3 us
    ppermute x6, waiting for transfers between devices, shift(): return lax.ppermute(array, 'cluster', [(i, (i + k) % n) for i in range(n)])  16.1 us
    all_to_all x2, starting transfers between devices, exchange(): return lax.all_to_all(field, 'tm', split_axis=0, concat_axis=0, tiled=True)  15 us
    pallas_call x2, Pallas kernels, band_apply(): pl.pallas_call(functools.partial(band_kernel, group), in_specs=[pl.BlockS...  9.25 us
    pallas_call x1, Pallas kernels, two_hops(): pl.pallas_call(hops_kernel, in_specs=[smem, smem, smem, hbm, hbm, hbm], o...  7.96 us
    ppermute x6, starting transfers between devices, shift(): return lax.ppermute(array, 'cluster', [(i, (i + k) % n) for i in range(n)])  7.22 us
    pallas_call x1, Pallas kernels, prepare(): pl.pallas_call(prepare_kernel, in_specs=[smem, smem, smem, vmem, vmem], o...  6.7 us
    dot_general x1, matrix products, on_device(): jnp.einsum('vf,vg->fg', propagated[0], dz, preferred_element_type=f32)  3.72 us
  transfers between devices with their start and end apart: 8, of which 8 were waited for; matrix products, arithmetic and copies ran while one was open for 7% of the time, Pallas kernels for 6%

profile of v3, /device:TPU:0, one launch (start us, length us, event | category | flops | bytes accessed | tf_op | source)
XLA Modules:
  0.0 116.6 jit_solution(6428607261785601653)
XLA Ops:
  0.6 0.0 copy-start
  0.6 4.8 %shard_map.96 = bf16[32,96,512]{2,1,0:T(8,128)(2,1)} custom-call(s32[32]{0:T(128)} %band_ref.3, bf16[32,96,512]{2,1,0:T(8,128)(2,1)} %field_hbm.1), custom_call_target="tpu_custom_call" | custom-call | tf_op jit(solution)/shard_map/pallas_call | solution.py:75
  5.4 7.5 %all-to-all-start = ((bf16[32,96,512]{2,1,0:T(8,128)(2,1)}), bf16[32,96,512]{2,1,0:T(8,128)(2,1)}, u32[]{:S(2)}, u32[]{:S(2)}) async-start(bf16[32,96,512]{2,1,0:T(8,128)(2,1)} %shard_map.96), calls=%async_computation | async-start | bytes 6291456 | tf_op jit(solution)/shard_map/all_to_all | solution.py:270
  13.6 6.7 %shard_map.95 = (bf16[160,128,128]{2,1,0:T(8,128)(2,1)}, s32[160]{0:T(256)}, s32[80]{0:T(128)}, s32[1]{0:T(128)}, bf16[512,512]{1,0:T(8,128)(2,1)}) custom-call(s32[128]{0:T(128)} %bitcast.38, s32[128]{0:T(128)} %bitcast.39, s32[1]{0:T(128)} %bitcast.29.count_ref, bf16[128,128,128]{2,1,0:T(8,128)(2,1)} %bitcast.31, bf16[512,512]{1,0:T(8,128)(2,1)} %bitcast.35), custom_call_target="tpu_custom_call" | custom-call | tf_op jit(solution)/shard_map/pallas_call | solution.py:139
  20.3 34.4 %all-to-all-done = bf16[32,96,512]{2,1,0:T(8,128)(2,1)} async-done(((bf16[32,96,512]{2,1,0:T(8,128)(2,1)}), bf16[32,96,512]{2,1,0:T(8,128)(2,1)}, u32[]{:S(2)}, u32[]{:S(2)}) %all-to-all-start) | async-done | bytes 3145760 | tf_op jit(solution)/shard_map/all_to_all | solution.py:270
  54.7 8.0 %shard_map.97 = bf16[3072,512]{1,0:T(8,128)(2,1)} custom-call(s32[160]{0:T(256)} %get-tuple-element.7.slot_rows_ref, s32[80]{0:T(128)} %get-tuple-element.8.slot_cols_ref, s32[1]{0:T(128)} %get-tuple-element.9.slots_ref, bf16[3072,512]{1,0:T(8,128)(2,1)} %bitcast.5.dz_hbm, bf16[512,512]{1,0:T(8,128)(2,1)} %get-tuple-element.10.weight_hbm, ...), custom_call_target="tpu_custom_call" | custom-call | tf_op jit(solution)/shard_map/pallas_call | solution.py:248
  62.7 7.5 %all-to-all-start.1 = ((bf16[32,96,512]{2,1,0:T(8,128)(2,1)}), bf16[32,96,512]{2,1,0:T(8,128)(2,1)}, u32[]{:S(2)}, u32[]{:S(2)}) async-start(bf16[32,96,512]{2,1,0:T(8,128)(2,1)} %bitcast.30), calls=%async_computation.1 | async-start | bytes 6291456 | tf_op jit(solution)/shard_map/all_to_all | solution.py:270
  70.2 0.0 copy-done
  70.2 3.7 %fusion.2 = bf16[512,512]{0,1:T(8,128)(2,1)S(1)} fusion(bf16[3072,512]{1,0:T(8,128)(2,1)} %bitcast.5.dz_hbm, bf16[1,3072,512]{2,1,0:T(8,128)(2,1)S(1)} %copy-done), kind=kOutput, calls=%fused_computation.2 | convolution fusion | flops 1610874880 | bytes 6815744 | tf_op jit(solution)/shard_map/vf,vg->fg/dot_general | solution.py:303
  73.9 0.0 copy-start.1
  73.9 0.8 copy-done.1
  74.7 0.7 dynamic-slice_bitcast_fusion.2
  75.5 4.1 %collective-permute-start.2 = (bf16[128,512]{1,0:T(8,128)(2,1)}, bf16[128,512]{1,0:T(8,128)(2,1)S(1)}, u32[]{:S(2)}, u32[]{:S(2)}) collective-permute-start(bf16[128,512]{1,0:T(8,128)(2,1)} %get-tuple-element.17), channel_id=1, source_target_pairs={{0,3},{1,0},{2,1},{3,2},{4,7},{5,4},{6,5},{7,6},{8,11},{9,8},{10,9... | collective-permute-start | bytes 393224 | tf_op jit(solution)/shard_map/ppermute | solution.py:278
  79.5 0.0 collective-permute-start.1
  79.5 0.9 collective-permute-start
  80.4 5.4 %collective-permute-done.2 = bf16[128,512]{1,0:T(8,128)(2,1)S(1)} collective-permute-done((bf16[128,512]{1,0:T(8,128)(2,1)}, bf16[128,512]{1,0:T(8,128)(2,1)S(1)}, u32[]{:S(2)}, u32[]{:S(2)}) %collective-permute-start.2) | collective-permute-done | bytes 131104 | tf_op jit(solution)/shard_map/ppermute | solution.py:278
  85.8 1.8 %collective-permute-done.1 = bf16[128,512]{1,0:T(8,128)(2,1)S(1)} collective-permute-done((bf16[128,512]{1,0:T(8,128)(2,1)}, bf16[128,512]{1,0:T(8,128)(2,1)S(1)}, u32[]{:S(2)}, u32[]{:S(2)}) %collective-permute-start.1) | collective-permute-done | bytes 131104 | tf_op jit(solution)/shard_map/ppermute | solution.py:278
  87.6 1.4 %collective-permute-done = bf16[128,512]{1,0:T(8,128)(2,1)} collective-permute-done((bf16[128,512]{1,0:T(8,128)(2,1)S(1)}, bf16[128,512]{1,0:T(8,128)(2,1)}, u32[]{:S(2)}, u32[]{:S(2)}) %collective-permute-start) | collective-permute-done | bytes 131104 | tf_op jit(solution)/shard_map/ppermute | solution.py:278
  89.0 1.0 fusion.7
  90.0 1.2 %collective-permute-start.5 = (bf16[128,512]{1,0:T(8,128)(2,1)S(1)}, bf16[128,512]{1,0:T(8,128)(2,1)S(1)}, u32[]{:S(2)}, u32[]{:S(2)}) collective-permute-start(bf16[128,512]{1,0:T(8,128)(2,1)S(1)} %fusion.7), channel_id=1, source_target_pairs={{0,3},{1,0},{2,1},{3,2},{4,7},{5,4},{6,5},{7,6},{8,11},{9,8},{10,9... | collective-permute-start | bytes 393224 | tf_op jit(solution)/shard_map/ppermute | solution.py:278
  91.2 0.2 collective-permute-start.4
  91.4 0.9 collective-permute-start.3
  92.3 4.1 %collective-permute-done.5 = bf16[128,512]{1,0:T(8,128)(2,1)S(1)} collective-permute-done((bf16[128,512]{1,0:T(8,128)(2,1)S(1)}, bf16[128,512]{1,0:T(8,128)(2,1)S(1)}, u32[]{:S(2)}, u32[]{:S(2)}) %collective-permute-start.5) | collective-permute-done | bytes 131104 | tf_op jit(solution)/shard_map/ppermute | solution.py:278
  96.4 2.2 %collective-permute-done.4 = bf16[128,512]{1,0:T(8,128)(2,1)S(1)} collective-permute-done((bf16[128,512]{1,0:T(8,128)(2,1)S(1)}, bf16[128,512]{1,0:T(8,128)(2,1)S(1)}, u32[]{:S(2)}, u32[]{:S(2)}) %collective-permute-start.4) | collective-permute-done | bytes 131104 | tf_op jit(solution)/shard_map/ppermute | solution.py:278
  98.6 1.3 %collective-permute-done.3 = bf16[128,512]{1,0:T(8,128)(2,1)} collective-permute-done((bf16[128,512]{1,0:T(8,128)(2,1)S(1)}, bf16[128,512]{1,0:T(8,128)(2,1)}, u32[]{:S(2)}, u32[]{:S(2)}) %collective-permute-start.3) | collective-permute-done | bytes 131104 | tf_op jit(solution)/shard_map/ppermute | solution.py:278
  99.9 1.0 pad_maximum_fusion
  100.9 1.1 maximum_convert_fusion
  102.0 9.9 %all-to-all-done.1.field_hbm = bf16[32,96,512]{2,1,0:T(8,128)(2,1)} async-done(((bf16[32,96,512]{2,1,0:T(8,128)(2,1)}), bf16[32,96,512]{2,1,0:T(8,128)(2,1)}, u32[]{:S(2)}, u32[]{:S(2)}) %all-to-all-start.1) | async-done | bytes 3145760 | tf_op jit(solution)/shard_map/all_to_all | solution.py:270
  111.9 4.5 %shard_map.98 = bf16[32,96,512]{2,1,0:T(8,128)(2,1)} custom-call(s32[32]{0:T(128)} %band_ref.3, bf16[32,96,512]{2,1,0:T(8,128)(2,1)} %all-to-all-done.1.field_hbm), custom_call_target="tpu_custom_call" | custom-call | tf_op jit(solution)/shard_map/pallas_call | solution.py:75
  (1 shorter events, 0.0 us)
Async XLA Ops:
  0.6 69.6 %copy-start = (bf16[1,3072,512]{2,1,0:T(8,128)(2,1)S(1)}, bf16[1,3072,512]{2,1,0:T(8,128)(2,1)}, u32[]{:S(2)}) copy-start(bf16[1,3072,512]{2,1,0:T(8,128)(2,1)} %param.9) | copy-start | bytes 9437188
  5.4 49.3 %all-to-all-start = ((bf16[32,96,512]{2,1,0:T(8,128)(2,1)}), bf16[32,96,512]{2,1,0:T(8,128)(2,1)}, u32[]{:S(2)}, u32[]{:S(2)}) async-start(bf16[32,96,512]{2,1,0:T(8,128)(2,1)} %shard_map.96), calls=%async_computation | async-start | bytes 6291456 | tf_op jit(solution)/shard_map/all_to_all | solution.py:270
  62.7 49.2 %all-to-all-start.1 = ((bf16[32,96,512]{2,1,0:T(8,128)(2,1)}), bf16[32,96,512]{2,1,0:T(8,128)(2,1)}, u32[]{:S(2)}, u32[]{:S(2)}) async-start(bf16[32,96,512]{2,1,0:T(8,128)(2,1)} %bitcast.30), calls=%async_computation.1 | async-start | bytes 6291456 | tf_op jit(solution)/shard_map/all_to_all | solution.py:270
  73.9 0.8 copy-start.1
  75.5 10.3 %collective-permute-start.2 = (bf16[128,512]{1,0:T(8,128)(2,1)}, bf16[128,512]{1,0:T(8,128)(2,1)S(1)}, u32[]{:S(2)}, u32[]{:S(2)}) collective-permute-start(bf16[128,512]{1,0:T(8,128)(2,1)} %get-tuple-element.17), channel_id=1, source_target_pairs={{0,3},{1,0},{2,1},{3,2},{4,7},{5,4},{6,5},{7,6},{8,11},{9,8},{10,9... | collective-permute-start | bytes 393224 | tf_op jit(solution)/shard_map/ppermute | solution.py:278
  79.5 8.1 %collective-permute-start.1 = (bf16[128,512]{1,0:T(8,128)(2,1)}, bf16[128,512]{1,0:T(8,128)(2,1)S(1)}, u32[]{:S(2)}, u32[]{:S(2)}) collective-permute-start(bf16[128,512]{1,0:T(8,128)(2,1)} %get-tuple-element.18), channel_id=1, source_target_pairs={{0,2},{1,3},{2,0},{3,1},{4,6},{5,7},{6,4},{7,5},{8,10},{9,11},{10,... | collective-permute-start | bytes 393224 | tf_op jit(solution)/shard_map/ppermute | solution.py:278
  79.5 9.5 %collective-permute-start = (bf16[128,512]{1,0:T(8,128)(2,1)S(1)}, bf16[128,512]{1,0:T(8,128)(2,1)}, u32[]{:S(2)}, u32[]{:S(2)}) collective-permute-start(bf16[128,512]{1,0:T(8,128)(2,1)S(1)} %get-tuple-element.16), channel_id=1, source_target_pairs={{0,1},{1,2},{2,3},{3,0},{4,5},{5,6},{6,7},{7,4},{8,9},{9,10},{10,1... | collective-permute-start | bytes 393224 | tf_op jit(solution)/shard_map/ppermute | solution.py:278
  90.0 6.4 %collective-permute-start.5 = (bf16[128,512]{1,0:T(8,128)(2,1)S(1)}, bf16[128,512]{1,0:T(8,128)(2,1)S(1)}, u32[]{:S(2)}, u32[]{:S(2)}) collective-permute-start(bf16[128,512]{1,0:T(8,128)(2,1)S(1)} %fusion.7), channel_id=1, source_target_pairs={{0,3},{1,0},{2,1},{3,2},{4,7},{5,4},{6,5},{7,6},{8,11},{9,8},{10,9... | collective-permute-start | bytes 393224 | tf_op jit(solution)/shard_map/ppermute | solution.py:278
  91.2 7.4 %collective-permute-start.4 = (bf16[128,512]{1,0:T(8,128)(2,1)S(1)}, bf16[128,512]{1,0:T(8,128)(2,1)S(1)}, u32[]{:S(2)}, u32[]{:S(2)}) collective-permute-start(bf16[128,512]{1,0:T(8,128)(2,1)S(1)} %fusion.7), channel_id=1, source_target_pairs={{0,2},{1,3},{2,0},{3,1},{4,6},{5,7},{6,4},{7,5},{8,10},{9,11},{10,... | collective-permute-start | bytes 393224 | tf_op jit(solution)/shard_map/ppermute | solution.py:278
  91.4 8.4 %collective-permute-start.3 = (bf16[128,512]{1,0:T(8,128)(2,1)S(1)}, bf16[128,512]{1,0:T(8,128)(2,1)}, u32[]{:S(2)}, u32[]{:S(2)}) collective-permute-start(bf16[128,512]{1,0:T(8,128)(2,1)S(1)} %fusion.7), channel_id=1, source_target_pairs={{0,1},{1,2},{2,3},{3,0},{4,5},{5,6},{6,7},{7,4},{8,9},{9,10},{10,1... | collective-permute-start | bytes 393224 | tf_op jit(solution)/shard_map/ppermute | solution.py:278

commit v4 on v3

--- a/solution.py
+++ b/solution.py
@@ -16,21 +16,18 @@
 VMEM_LIMIT = 56 * 2**20
 
 
-def band_kernel(group, band_ref, field_hbm, out_hbm, field, out, in_sems, out_sems):
+def band_kernel(group, band_ref, field, out_hbm, out, out_sems, pull=None):
     total, verts, width = field.shape
     groups = total // group
     rows, lanes = 16, 256
 
-    def pull(g):
-        part = pl.ds(g * group, group)
-        return pltpu.make_async_copy(field_hbm.at[part], field.at[part], in_sems.at[g])
-
     def push(g):
         part = pl.ds(g * group, group)
         return pltpu.make_async_copy(out.at[part], out_hbm.at[part], out_sems.at[g])
 
-    for g in range(groups):
-        pull(g).start()
+    if pull is not None:
+        for g in range(groups):
+            pull(g).start()
     widths = [band_ref[t] for t in range(total)]
     scales = [
         jnp.where(
@@ -40,9 +37,10 @@
         )
         for width in widths
     ]
-    pull(0).wait()
+    if pull is not None:
+        pull(0).wait()
     for g in range(groups):
-        if g + 1 < groups:
+        if pull is not None and g + 1 < groups:
             pull(g + 1).wait()
         start = g * group
         stop = min(start + group + BAND - 1, total)
@@ -69,32 +67,43 @@
         push(g).wait()
 
 
-def band_apply(band, field, group=4):
+def band_pull_kernel(group, band_ref, field_hbm, out_hbm, field, in_sems, out, out_sems):
+    def pull(g):
+        part = pl.ds(g * group, group)
+        return pltpu.make_async_copy(field_hbm.at[part], field.at[part], in_sems.at[g])
+
+    band_kernel(group, band_ref, field, out_hbm, out, out_sems, pull)
+
+
+def band_apply(band, field, resident, group=4):
     total = field.shape[0]
     hbm = pl.BlockSpec(memory_space=pltpu.HBM)
+    vmem = pl.BlockSpec(memory_space=pltpu.VMEM)
+    staged = [pltpu.VMEM(field.shape, bf16), pltpu.SemaphoreType.DMA((total // group,))]
     return pl.pallas_call(
-        functools.partial(band_kernel, group),
-        in_specs=[pl.BlockSpec(memory_space=pltpu.SMEM), hbm],
+        functools.partial(band_kernel if resident else band_pull_kernel, group),
+        in_specs=[pl.BlockSpec(memory_space=pltpu.SMEM), vmem if resident else hbm],
         out_specs=hbm,
         out_shape=jax.ShapeDtypeStruct(field.shape, bf16),
-        scratch_shapes=[
-            pltpu.VMEM(field.shape, bf16),
-            pltpu.VMEM(field.shape, bf16),
-            pltpu.SemaphoreType.DMA((total // group,)),
-            pltpu.SemaphoreType.DMA((total // group,)),
-        ],
-        compiler_params=pltpu.CompilerParams(vmem_limit_bytes=VMEM_LIMIT),
+        scratch_shapes=staged * (1 if resident else 2),
+        compiler_params=pltpu.CompilerParams(vmem_limit_bytes=(16 * 2**20 if resident else VMEM_LIMIT)),
     )(band, field)
 
 
 def prepare_kernel(
-    rows_ref, cols_ref, count_ref, values_ref, weight_ref,
-    tiles_ref, slot_rows_ref, slot_cols_ref, slots_ref, weight_t_ref, sizes, used,
+    rows_ref, cols_ref, count_ref, values_hbm, weight_hbm,
+    tiles_ref, slot_rows_ref, slot_cols_ref, slots_ref, weight_t_ref,
+    values_ref, weight_ref, sizes, used, values_sem, weight_sem,
 ):
     col_tiles = sizes.shape[0]
     slot_total = slot_cols_ref.shape[0]
     count = count_ref[0]
+    pull_weight = pltpu.make_async_copy(weight_hbm, weight_ref, weight_sem)
+    pull_values = pltpu.make_async_copy(values_hbm, values_ref, values_sem)
+    pull_weight.start()
+    pull_values.start()
     tiles_ref[...] = jnp.zeros_like(tiles_ref)
+    pull_weight.wait()
     weight_t_ref[...] = weight_ref[...].T
 
     def clear(s, carry):
@@ -128,6 +137,7 @@
         tiles_ref[half] = values_ref[b].T
         return carry
 
+    pull_values.wait()
     lax.fori_loop(0, count, place, 0)
 
 
@@ -136,9 +146,10 @@
     slot_total = -(-(blocks // 2 + col_tiles // 2) // SHORT) * SHORT
     smem = pl.BlockSpec(memory_space=pltpu.SMEM)
     vmem = pl.BlockSpec(memory_space=pltpu.VMEM)
+    hbm = pl.BlockSpec(memory_space=pltpu.HBM)
     return pl.pallas_call(
         prepare_kernel,
-        in_specs=[smem, smem, smem, vmem, vmem],
+        in_specs=[smem, smem, smem, hbm, hbm],
         out_specs=(vmem, smem, smem, smem, vmem),
         out_shape=(
             jax.ShapeDtypeStruct((2 * slot_total, BLK, BLK), bf16),
@@ -148,25 +159,25 @@
             jax.ShapeDtypeStruct(weight.shape, bf16),
         ),
         scratch_shapes=[
+            pltpu.VMEM(values.shape, bf16),
+            pltpu.VMEM(weight.shape, bf16),
             pltpu.SMEM((col_tiles,), jnp.int32),
             pltpu.SMEM((col_tiles,), jnp.int32),
+            pltpu.SemaphoreType.DMA,
+            pltpu.SemaphoreType.DMA,
         ],
         compiler_params=pltpu.CompilerParams(vmem_limit_bytes=VMEM_LIMIT),
     )(rows, cols, count, values, weight)
 
 
 def hops_kernel(
-    slot_rows_ref, slot_cols_ref, slots_ref, dz_hbm, weight_hbm, tiles_hbm, out_hbm,
-    dz, weight_t, tiles_ref, feats, first, second, weight_sem, dz_sems, tile_sems, out_sems,
+    slot_rows_ref, slot_cols_ref, slots_ref, dz, weight_hbm, tiles_hbm, out_hbm, dz_hbm,
+    out, weight_t, tiles_ref, feats, first, second, weight_sem, tile_sems, out_sem, dz_sem,
 ):
     tiles = feats.shape[0]
-    group = tiles // dz_sems.shape[0]
+    group = tiles // 2
     units = (slots_ref[0] + SHORT - 1) // SHORT
     trips = units // (LONG // SHORT)
-
-    def pull(k):
-        part = pl.ds(k * group * BLK, group * BLK)
-        return pltpu.make_async_copy(dz_hbm.at[part], dz.at[part], dz_sems.at[k])
 
     def pull_tiles(q):
         part = pl.ds(q * 2 * SHORT, 2 * SHORT)
@@ -174,7 +185,7 @@
 
     def push(c):
         part = pl.ds(pl.multiple_of(c * BLK, BLK), BLK)
-        return pltpu.make_async_copy(dz.at[part], out_hbm.at[part], out_sems.at[c])
+        return pltpu.make_async_copy(out.at[part], out_hbm.at[part], out_sem)
 
     def start_tiles(q, carry):
         pull_tiles(q).start()
@@ -182,15 +193,13 @@
 
     pull_weight = pltpu.make_async_copy(weight_hbm, weight_t, weight_sem)
     pull_weight.start()
-    for k in range(tiles // group):
-        pull(k).start()
+    lax.fori_loop(0, units, start_tiles, 0)
+    keep_dz = pltpu.make_async_copy(dz, dz_hbm, dz_sem)
+    keep_dz.start()
     first[...] = jnp.zeros_like(first)
     second[...] = jnp.zeros_like(second)
     pull_weight.wait()
     for k in range(tiles // group):
-        pull(k).wait()
-        if k == 0:
-            lax.fori_loop(0, units, start_tiles, 0)
         pushed = jnp.dot(
             dz[k * group * BLK : (k + 1) * group * BLK, :], weight_t[...], preferred_element_type=f32
         ).astype(bf16)
@@ -208,7 +217,7 @@
             acc[c] = acc[c] + jnp.dot(left, right, preferred_element_type=f32)
 
     def finish(c, carry):
-        dz[pl.ds(pl.multiple_of(c * BLK, BLK), BLK), :] = second[c].astype(bf16)
+        out[pl.ds(pl.multiple_of(c * BLK, BLK), BLK), :] = second[c].astype(bf16)
         push(c).start()
         return carry
 
@@ -235,21 +244,20 @@
     feats[...] = first[...].astype(bf16)
     done = lax.fori_loop(0, trips, functools.partial(second_hop, LONG), jnp.int32(0))
     lax.fori_loop(rest, units, functools.partial(second_hop, SHORT), done)
-    for c in range(tiles):
-        push(c).wait()
+    keep_dz.wait()
+    pltpu.make_async_copy(out, out_hbm, out_sem).wait()
 
 
 def two_hops(slot_rows, slot_cols, slots, dz, weight_t, tiles):
     verts, width = dz.shape
     col_tiles = verts // BLK
-    parts = 2
     smem = pl.BlockSpec(memory_space=pltpu.SMEM)
     hbm = pl.BlockSpec(memory_space=pltpu.HBM)
     return pl.pallas_call(
         hops_kernel,
-        in_specs=[smem, smem, smem, hbm, hbm, hbm],
-        out_specs=hbm,
-        out_shape=jax.ShapeDtypeStruct((verts, width), bf16),
+        in_specs=[smem, smem, smem, pl.BlockSpec(memory_space=pltpu.VMEM), hbm, hbm],
+        out_specs=(hbm, hbm),
+        out_shape=(pltpu.HBM((verts, width), bf16),) * 2,
         scratch_shapes=[
             pltpu.VMEM((verts, width), bf16),
             pltpu.VMEM(weight_t.shape, bf16),
@@ -258,12 +266,41 @@
             pltpu.VMEM((col_tiles, BLK, width), f32),
             pltpu.VMEM((col_tiles, BLK, width), f32),
             pltpu.SemaphoreType.DMA,
-            pltpu.SemaphoreType.DMA((parts,)),
             pltpu.SemaphoreType.DMA((tiles.shape[0] // (2 * SHORT),)),
-            pltpu.SemaphoreType.DMA((col_tiles,)),
+            pltpu.SemaphoreType.DMA,
+            pltpu.SemaphoreType.DMA,
+        ],
+        compiler_params=pltpu.CompilerParams(vmem_limit_bytes=48 * 2**20),
+    )(slot_rows, slot_cols, slots, dz, weight_t, tiles)
+
+
+def terms_kernel(left_hbm, right_hbm, out_ref, left, right, left_sem, right_sem):
+    pull_left = pltpu.make_async_copy(left_hbm, left, left_sem)
+    pull_right = pltpu.make_async_copy(right_hbm, right, right_sem)
+    pull_left.start()
+    pull_right.start()
+    pull_left.wait()
+    pull_right.wait()
+    out_ref[...] = lax.dot_general(
+        left[...], right[...], (((0,), (0,)), ((), ())), preferred_element_type=f32
+    ).astype(bf16)
+
+
+def gradient_terms(left, right):
+    hbm = pl.BlockSpec(memory_space=pltpu.HBM)
+    return pl.pallas_call(
+        terms_kernel,
+        in_specs=[hbm, hbm],
+        out_specs=pl.BlockSpec(memory_space=pltpu.VMEM),
+        out_shape=jax.ShapeDtypeStruct((left.shape[1], right.shape[1]), bf16),
+        scratch_shapes=[
+            pltpu.VMEM(left.shape, bf16),
+            pltpu.VMEM(right.shape, bf16),
+            pltpu.SemaphoreType.DMA,
+            pltpu.SemaphoreType.DMA,
         ],
         compiler_params=pltpu.CompilerParams(vmem_limit_bytes=VMEM_LIMIT),
-    )(slot_rows, slot_cols, slots, dz, weight_t, tiles)
+    )(left, right)
 
 
 def exchange(field):
@@ -272,7 +309,7 @@
 
 def cluster_sum(terms, n):
     me = lax.axis_index("cluster")
-    parts = terms.astype(bf16).reshape(n, terms.shape[0] // n, terms.shape[1])
+    parts = terms.reshape(n, terms.shape[0] // n, terms.shape[1])
 
     def shift(array, k):
         return lax.ppermute(array, "cluster", [(i, (i + k) % n) for i in range(n)])
@@ -294,13 +331,13 @@
 ):
     snaps, own, width = cotangent.shape
     verts = snaps * own
-    dz = exchange(band_apply(band, cotangent)).reshape(verts, width)
+    dz = exchange(band_apply(band, cotangent, False)).reshape(verts, width)
     tiles, slot_rows, slot_cols, slots, weight_t = prepare(
         block_rows[0, 0], block_cols[0, 0], block_counts[0], block_values[0, 0], weight[0], verts // BLK
     )
-    second = two_hops(slot_rows, slot_cols, slots, dz, weight_t, tiles)
-    input_grad = band_apply(band, exchange(second.reshape(snaps, own, width)))
-    terms = jnp.einsum("vf,vg->fg", propagated[0], dz, preferred_element_type=f32)
+    second, dz = two_hops(slot_rows, slot_cols, slots, dz, weight_t, tiles)
+    input_grad = band_apply(band, exchange(second.reshape(snaps, own, width)), True)
+    terms = gradient_terms(propagated[0], dz)
     weight_grad = cluster_sum(terms, n_cluster)
     return (input_grad, weight_grad[None])
 

time: 117 us -> 116 us (level)
  matrix products: 3.72 us -> 0 us
  local copies, waits for them, and re-layouts: 1.57 us -> 4.16 us
  Pallas kernels: 23.9 us -> 25.7 us
  waiting for transfers between devices: 60.5 us -> 59.2 us
    dot_general x1 -> x0, matrix products: 3.72 us -> none  [on_device(): jnp.einsum('vf,vg->fg', propagated[0], dz, preferred_element_type=f32)]
    pallas_call x4 -> x5, Pallas kernels: 23.9 us -> 25.7 us  [the longest x2 7.64 us: band_apply(): pl.pallas_call(functools.partial(band_kernel if resident else band_pull_k...]
    unnamed x4 -> x8, local copies, waits for them, and re-layouts: 0.8 us -> 2.36 us
    all_to_all x2, waiting for transfers between devices: 44.3 us -> 43 us  [exchange(): return lax.all_to_all(field, 'tm', split_axis=0, concat_axis=0, tiled=True)]
  transfers between devices with their start and end apart: 8 -> 8, of which waited for: 8 -> 8; matrix products, arithmetic and copies ran while one was open for 7% -> 4% of each run, Pallas kernels for 6% -> 10%
where the time goes in v4:
time: 116 us
  waiting for transfers between devices  59.2 us (51%)
  Pallas kernels  25.7 us (22%)
  starting transfers between devices  22.2 us (19%)
  local copies, waits for them, and re-layouts  4.16 us (4%)
  other arithmetic  3.11 us (3%)
  between operations  1.56 us (1%)
    all_to_all x2, waiting for transfers between devices, exchange(): return lax.all_to_all(field, 'tm', split_axis=0, concat_axis=0, tiled=True)  43 us
    ppermute x6, waiting for transfers between devices, shift(): return lax.ppermute(array, 'cluster', [(i, (i + k) % n) for i in range(n)])  16.2 us
    all_to_all x2, starting transfers between devices, exchange(): return lax.all_to_all(field, 'tm', split_axis=0, concat_axis=0, tiled=True)  14.8 us
    pallas_call x2, Pallas kernels, band_apply(): pl.pallas_call(functools.partial(band_kernel if resident else band_pull_k...  7.64 us
    ppermute x6, starting transfers between devices, shift(): return lax.ppermute(array, 'cluster', [(i, (i + k) % n) for i in range(n)])  7.42 us
    pallas_call x1, Pallas kernels, two_hops(): pl.pallas_call(hops_kernel, in_specs=[smem, smem, smem, pl.BlockSpec(memo...  6.8 us
    pallas_call x1, Pallas kernels, prepare(): pl.pallas_call(prepare_kernel, in_specs=[smem, smem, smem, hbm, hbm], out...  5.79 us
    pallas_call x1, Pallas kernels, gradient_terms(): pl.pallas_call(terms_kernel, in_specs=[hbm, hbm], out_specs=pl.BlockSpec(...  5.47 us
  transfers between devices with their start and end apart: 8, of which 8 were waited for; matrix products, arithmetic and copies ran while one was open for 4% of the time, Pallas kernels for 10%

profile of v4, /device:TPU:0, one launch (start us, length us, event | category | flops | bytes accessed | tf_op | source)
XLA Modules:
  0.0 115.9 jit_solution(13978670959287361840)
XLA Ops:
  0.6 4.5 %shard_map.96 = bf16[32,96,512]{2,1,0:T(8,128)(2,1)} custom-call(s32[32]{0:T(128)} %band_ref.3, bf16[32,96,512]{2,1,0:T(8,128)(2,1)} %field_hbm.1), custom_call_target="tpu_custom_call" | custom-call | tf_op jit(solution)/shard_map/pallas_call | solution.py:83
  5.1 7.4 %all-to-all-start = ((bf16[32,96,512]{2,1,0:T(8,128)(2,1)}), bf16[32,96,512]{2,1,0:T(8,128)(2,1)S(1)}, u32[]{:S(2)}, u32[]{:S(2)}) async-start(bf16[32,96,512]{2,1,0:T(8,128)(2,1)} %shard_map.96), calls=%async_computation | async-start | bytes 6291456 | tf_op jit(solution)/shard_map/all_to_all | solution.py:307
  13.2 5.8 %shard_map.95 = (bf16[160,128,128]{2,1,0:T(8,128)(2,1)}, s32[160]{0:T(256)}, s32[80]{0:T(128)}, s32[1]{0:T(128)}, bf16[512,512]{1,0:T(8,128)(2,1)}) custom-call(s32[128]{0:T(128)} %bitcast.33, s32[128]{0:T(128)} %bitcast.34, s32[1]{0:T(128)} %bitcast.22.count_ref, bf16[128,128,128]{2,1,0:T(8,128)(2,1)} %bitcast.24, bf16[512,512]{1,0:T(8,128)(2,1)} %bitcast.30), custom_call_target="tpu_custom_call" | custom-call | tf_op jit(solution)/shard_map/pallas_call | solution.py:150
  19.0 35.3 %all-to-all-done = bf16[32,96,512]{2,1,0:T(8,128)(2,1)S(1)} async-done(((bf16[32,96,512]{2,1,0:T(8,128)(2,1)}), bf16[32,96,512]{2,1,0:T(8,128)(2,1)S(1)}, u32[]{:S(2)}, u32[]{:S(2)}) %all-to-all-start) | async-done | bytes 3145760 | tf_op jit(solution)/shard_map/all_to_all | solution.py:307
  54.3 0.0 copy-start
  54.3 1.0 copy-done
  55.4 0.0 copy-start.2
  55.4 0.6 copy-done.2
  56.0 0.0 copy-start.3
  56.0 0.7 copy-done.3
  56.7 6.8 %shard_map.97 = (bf16[3072,512]{1,0:T(8,128)(2,1)}, bf16[3072,512]{1,0:T(8,128)(2,1)}) custom-call(s32[160]{0:T(256)S(1)} %copy-done.2, s32[80]{0:T(128)S(1)} %copy-done.3, s32[1]{0:T(128)} %get-tuple-element.11.slots_ref, bf16[3072,512]{1,0:T(8,128)(2,1)S(1)} %bitcast.23, bf16[512,512]{1,0:T(8,128)(2,1)S(1)} %copy-done, ...), custom_call_target="tpu_custom_call" | custom-call | tf_op jit(solution)/shard_map/pallas_call | solution.py:256
  63.5 7.4 %all-to-all-start.1 = ((bf16[32,96,512]{2,1,0:T(8,128)(2,1)}), bf16[32,96,512]{2,1,0:T(8,128)(2,1)S(1)}, u32[]{:S(2)}, u32[]{:S(2)}) async-start(bf16[32,96,512]{2,1,0:T(8,128)(2,1)} %bitcast.25), calls=%async_computation.1 | async-start | bytes 6291456 | tf_op jit(solution)/shard_map/all_to_all | solution.py:307
  70.9 5.5 %shard_map.99 = bf16[512,512]{1,0:T(8,128)(2,1)} custom-call(bf16[3072,512]{1,0:T(8,128)(2,1)} %bitcast.26, bf16[3072,512]{1,0:T(8,128)(2,1)} %get-tuple-element.15.right_hbm), custom_call_target="tpu_custom_call" | custom-call | tf_op jit(solution)/shard_map/pallas_call | solution.py:291
  76.4 0.0 copy-start.1
  76.4 1.8 %dynamic-slice_bitcast_fusion.2 = (bf16[128,512]{1,0:T(8,128)(2,1)S(1)}, bf16[128,512]{1,0:T(8,128)(2,1)}, bf16[128,512]{1,0:T(8,128)(2,1)}) fusion(bf16[4,128,512]{2,1,0:T(8,128)(2,1)} %bitcast.27, s32[]{:T(128)S(6)} %select_n.51, s32[]{:T(128)S(6)} %select_n.55, s32[]{:T(128)S(6)} %select_n.53), kind=kLoop, calls=%fused_computation.8 | loop fusion | bytes 786444 | tf_op jit(solution)/shard_map/jit(dynamic_index_in_dim)/squeeze | solution.py:318
  78.1 4.1 %collective-permute-start.2 = (bf16[128,512]{1,0:T(8,128)(2,1)}, bf16[128,512]{1,0:T(8,128)(2,1)S(1)}, u32[]{:S(2)}, u32[]{:S(2)}) collective-permute-start(bf16[128,512]{1,0:T(8,128)(2,1)} %get-tuple-element.21), channel_id=1, source_target_pairs={{0,3},{1,0},{2,1},{3,2},{4,7},{5,4},{6,5},{7,6},{8,11},{9,8},{10,9... | collective-permute-start | bytes 393224 | tf_op jit(solution)/shard_map/ppermute | solution.py:315
  82.2 0.0 collective-permute-start.1
  82.2 0.9 collective-permute-start
  83.1 5.4 %collective-permute-done.2 = bf16[128,512]{1,0:T(8,128)(2,1)S(1)} collective-permute-done((bf16[128,512]{1,0:T(8,128)(2,1)}, bf16[128,512]{1,0:T(8,128)(2,1)S(1)}, u32[]{:S(2)}, u32[]{:S(2)}) %collective-permute-start.2) | collective-permute-done | bytes 131104 | tf_op jit(solution)/shard_map/ppermute | solution.py:315
  88.5 1.8 %collective-permute-done.1 = bf16[128,512]{1,0:T(8,128)(2,1)S(1)} collective-permute-done((bf16[128,512]{1,0:T(8,128)(2,1)}, bf16[128,512]{1,0:T(8,128)(2,1)S(1)}, u32[]{:S(2)}, u32[]{:S(2)}) %collective-permute-start.1) | collective-permute-done | bytes 131104 | tf_op jit(solution)/shard_map/ppermute | solution.py:315
  90.3 1.4 %collective-permute-done = bf16[128,512]{1,0:T(8,128)(2,1)} collective-permute-done((bf16[128,512]{1,0:T(8,128)(2,1)S(1)}, bf16[128,512]{1,0:T(8,128)(2,1)}, u32[]{:S(2)}, u32[]{:S(2)}) %collective-permute-start) | collective-permute-done | bytes 131104 | tf_op jit(solution)/shard_map/ppermute | solution.py:315
  91.7 1.0 fusion.2
  92.8 1.4 %collective-permute-start.5 = (bf16[128,512]{1,0:T(8,128)(2,1)S(1)}, bf16[128,512]{1,0:T(8,128)(2,1)S(1)}, u32[]{:S(2)}, u32[]{:S(2)}) collective-permute-start(bf16[128,512]{1,0:T(8,128)(2,1)S(1)} %fusion.2), channel_id=1, source_target_pairs={{0,3},{1,0},{2,1},{3,2},{4,7},{5,4},{6,5},{7,6},{8,11},{9,8},{10,9... | collective-permute-start | bytes 393224 | tf_op jit(solution)/shard_map/ppermute | solution.py:315
  94.1 0.2 collective-permute-start.4
  94.4 0.9 collective-permute-start.3
  95.2 4.1 %collective-permute-done.5 = bf16[128,512]{1,0:T(8,128)(2,1)S(1)} collective-permute-done((bf16[128,512]{1,0:T(8,128)(2,1)S(1)}, bf16[128,512]{1,0:T(8,128)(2,1)S(1)}, u32[]{:S(2)}, u32[]{:S(2)}) %collective-permute-start.5) | collective-permute-done | bytes 131104 | tf_op jit(solution)/shard_map/ppermute | solution.py:315
  99.4 2.2 %collective-permute-done.4 = bf16[128,512]{1,0:T(8,128)(2,1)S(1)} collective-permute-done((bf16[128,512]{1,0:T(8,128)(2,1)S(1)}, bf16[128,512]{1,0:T(8,128)(2,1)S(1)}, u32[]{:S(2)}, u32[]{:S(2)}) %collective-permute-start.4) | collective-permute-done | bytes 131104 | tf_op jit(solution)/shard_map/ppermute | solution.py:315
  101.6 1.3 %collective-permute-done.3 = bf16[128,512]{1,0:T(8,128)(2,1)} collective-permute-done((bf16[128,512]{1,0:T(8,128)(2,1)S(1)}, bf16[128,512]{1,0:T(8,128)(2,1)}, u32[]{:S(2)}, u32[]{:S(2)}) %collective-permute-start.3) | collective-permute-done | bytes 131104 | tf_op jit(solution)/shard_map/ppermute | solution.py:315
  102.8 1.0 pad_maximum_fusion
  103.9 1.1 maximum_convert_fusion
  105.0 7.6 %all-to-all-done.1.field = bf16[32,96,512]{2,1,0:T(8,128)(2,1)S(1)} async-done(((bf16[32,96,512]{2,1,0:T(8,128)(2,1)}), bf16[32,96,512]{2,1,0:T(8,128)(2,1)S(1)}, u32[]{:S(2)}, u32[]{:S(2)}) %all-to-all-start.1) | async-done | bytes 3145760 | tf_op jit(solution)/shard_map/all_to_all | solution.py:307
  112.6 0.0 copy-done.1
  112.6 3.2 %shard_map.98 = bf16[32,96,512]{2,1,0:T(8,128)(2,1)} custom-call(s32[32]{0:T(128)S(1)} %copy-done.1, bf16[32,96,512]{2,1,0:T(8,128)(2,1)S(1)} %all-to-all-done.1.field), custom_call_target="tpu_custom_call" | custom-call | tf_op jit(solution)/shard_map/pallas_call | solution.py:83
  (1 shorter events, 0.0 us)
Async XLA Ops:
  5.1 49.2 %all-to-all-start = ((bf16[32,96,512]{2,1,0:T(8,128)(2,1)}), bf16[32,96,512]{2,1,0:T(8,128)(2,1)S(1)}, u32[]{:S(2)}, u32[]{:S(2)}) async-start(bf16[32,96,512]{2,1,0:T(8,128)(2,1)} %shard_map.96), calls=%async_computation | async-start | bytes 6291456 | tf_op jit(solution)/shard_map/all_to_all | solution.py:307
  54.3 1.0 copy-start
  55.4 0.6 copy-start.2
  56.0 0.7 copy-start.3
  63.5 49.1 %all-to-all-start.1 = ((bf16[32,96,512]{2,1,0:T(8,128)(2,1)}), bf16[32,96,512]{2,1,0:T(8,128)(2,1)S(1)}, u32[]{:S(2)}, u32[]{:S(2)}) async-start(bf16[32,96,512]{2,1,0:T(8,128)(2,1)} %bitcast.25), calls=%async_computation.1 | async-start | bytes 6291456 | tf_op jit(solution)/shard_map/all_to_all | solution.py:307
  76.4 36.3 %copy-start.1 = (s32[32]{0:T(128)S(1)}, s32[32]{0:T(128)}, u32[]{:S(2)}) copy-start(s32[32]{0:T(128)} %band_ref.3) | copy-start | bytes 388
  78.1 10.4 %collective-permute-start.2 = (bf16[128,512]{1,0:T(8,128)(2,1)}, bf16[128,512]{1,0:T(8,128)(2,1)S(1)}, u32[]{:S(2)}, u32[]{:S(2)}) collective-permute-start(bf16[128,512]{1,0:T(8,128)(2,1)} %get-tuple-element.21), channel_id=1, source_target_pairs={{0,3},{1,0},{2,1},{3,2},{4,7},{5,4},{6,5},{7,6},{8,11},{9,8},{10,9... | collective-permute-start | bytes 393224 | tf_op jit(solution)/shard_map/ppermute | solution.py:315
  82.2 8.1 %collective-permute-start.1 = (bf16[128,512]{1,0:T(8,128)(2,1)}, bf16[128,512]{1,0:T(8,128)(2,1)S(1)}, u32[]{:S(2)}, u32[]{:S(2)}) collective-permute-start(bf16[128,512]{1,0:T(8,128)(2,1)} %get-tuple-element.22), channel_id=1, source_target_pairs={{0,2},{1,3},{2,0},{3,1},{4,6},{5,7},{6,4},{7,5},{8,10},{9,11},{10,... | collective-permute-start | bytes 393224 | tf_op jit(solution)/shard_map/ppermute | solution.py:315
  82.2 9.5 %collective-permute-start = (bf16[128,512]{1,0:T(8,128)(2,1)S(1)}, bf16[128,512]{1,0:T(8,128)(2,1)}, u32[]{:S(2)}, u32[]{:S(2)}) collective-permute-start(bf16[128,512]{1,0:T(8,128)(2,1)S(1)} %get-tuple-element.20), channel_id=1, source_target_pairs={{0,1},{1,2},{2,3},{3,0},{4,5},{5,6},{6,7},{7,4},{8,9},{9,10},{10,1... | collective-permute-start | bytes 393224 | tf_op jit(solution)/shard_map/ppermute | solution.py:315
  92.8 6.6 %collective-permute-start.5 = (bf16[128,512]{1,0:T(8,128)(2,1)S(1)}, bf16[128,512]{1,0:T(8,128)(2,1)S(1)}, u32[]{:S(2)}, u32[]{:S(2)}) collective-permute-start(bf16[128,512]{1,0:T(8,128)(2,1)S(1)} %fusion.2), channel_id=1, source_target_pairs={{0,3},{1,0},{2,1},{3,2},{4,7},{5,4},{6,5},{7,6},{8,11},{9,8},{10,9... | collective-permute-start | bytes 393224 | tf_op jit(solution)/shard_map/ppermute | solution.py:315
  94.1 7.4 %collective-permute-start.4 = (bf16[128,512]{1,0:T(8,128)(2,1)S(1)}, bf16[128,512]{1,0:T(8,128)(2,1)S(1)}, u32[]{:S(2)}, u32[]{:S(2)}) collective-permute-start(bf16[128,512]{1,0:T(8,128)(2,1)S(1)} %fusion.2), channel_id=1, source_target_pairs={{0,2},{1,3},{2,0},{3,1},{4,6},{5,7},{6,4},{7,5},{8,10},{9,11},{10,... | collective-permute-start | bytes 393224 | tf_op jit(solution)/shard_map/ppermute | solution.py:315
  94.4 8.5 %collective-permute-start.3 = (bf16[128,512]{1,0:T(8,128)(2,1)S(1)}, bf16[128,512]{1,0:T(8,128)(2,1)}, u32[]{:S(2)}, u32[]{:S(2)}) collective-permute-start(bf16[128,512]{1,0:T(8,128)(2,1)S(1)} %fusion.2), channel_id=1, source_target_pairs={{0,1},{1,2},{2,3},{3,0},{4,5},{5,6},{6,7},{7,4},{8,9},{9,10},{10,1... | collective-permute-start | bytes 393224 | tf_op jit(solution)/shard_map/ppermute | solution.py:315

commit v5 on v4

--- a/solution.py
+++ b/solution.py
@@ -90,13 +90,22 @@
     )(band, field)
 
 
+def split_table(table_ref, slot_total):
+    return (
+        table_ref.at[pl.ds(0, 2 * slot_total)],
+        table_ref.at[pl.ds(2 * slot_total, slot_total)],
+        table_ref.at[pl.ds(3 * slot_total, 1)],
+    )
+
+
 def prepare_kernel(
     rows_ref, cols_ref, count_ref, values_hbm, weight_hbm,
-    tiles_ref, slot_rows_ref, slot_cols_ref, slots_ref, weight_t_ref,
+    tiles_ref, table_ref, weight_t_ref,
     values_ref, weight_ref, sizes, used, values_sem, weight_sem,
 ):
     col_tiles = sizes.shape[0]
-    slot_total = slot_cols_ref.shape[0]
+    slot_total = tiles_ref.shape[0] // 2
+    slot_rows_ref, slot_cols_ref, slots_ref = split_table(table_ref, slot_total)
     count = count_ref[0]
     pull_weight = pltpu.make_async_copy(weight_hbm, weight_ref, weight_sem)
     pull_values = pltpu.make_async_copy(values_hbm, values_ref, values_sem)
@@ -150,12 +159,10 @@
     return pl.pallas_call(
         prepare_kernel,
         in_specs=[smem, smem, smem, hbm, hbm],
-        out_specs=(vmem, smem, smem, smem, vmem),
+        out_specs=(vmem, smem, vmem),
         out_shape=(
             jax.ShapeDtypeStruct((2 * slot_total, BLK, BLK), bf16),
-            jax.ShapeDtypeStruct((2 * slot_total,), jnp.int32),
-            jax.ShapeDtypeStruct((slot_total,), jnp.int32),
-            jax.ShapeDtypeStruct((1,), jnp.int32),
+            jax.ShapeDtypeStruct((3 * slot_total + 1,), jnp.int32),
             jax.ShapeDtypeStruct(weight.shape, bf16),
         ),
         scratch_shapes=[
@@ -171,11 +178,13 @@
 
 
 def hops_kernel(
-    slot_rows_ref, slot_cols_ref, slots_ref, dz, weight_hbm, tiles_hbm, out_hbm, dz_hbm,
+    table_ref, dz, weight_hbm, tiles_hbm, out_hbm, dz_hbm,
     out, weight_t, tiles_ref, feats, first, second, weight_sem, tile_sems, out_sem, dz_sem,
 ):
     tiles = feats.shape[0]
     group = tiles // 2
+    slot_total = tiles_ref.shape[0] // 2
+    slot_rows_ref, slot_cols_ref, slots_ref = split_table(table_ref, slot_total)
     units = (slots_ref[0] + SHORT - 1) // SHORT
     trips = units // (LONG // SHORT)
 
@@ -232,7 +241,7 @@
         after = (q + 1) * length
         upto = jnp.where(
             after < units * SHORT,
-            slot_cols_ref[jnp.minimum(after, slot_cols_ref.shape[0] - 1)],
+            slot_cols_ref[jnp.minimum(after, slot_total - 1)],
             tiles,
         )
         lax.fori_loop(done, upto, finish, 0)
@@ -248,14 +257,14 @@
     pltpu.make_async_copy(out, out_hbm, out_sem).wait()
 
 
-def two_hops(slot_rows, slot_cols, slots, dz, weight_t, tiles):
+def two_hops(table, dz, weight_t, tiles):
     verts, width = dz.shape
     col_tiles = verts // BLK
     smem = pl.BlockSpec(memory_space=pltpu.SMEM)
     hbm = pl.BlockSpec(memory_space=pltpu.HBM)
     return pl.pallas_call(
         hops_kernel,
-        in_specs=[smem, smem, smem, pl.BlockSpec(memory_space=pltpu.VMEM), hbm, hbm],
+        in_specs=[smem, pl.BlockSpec(memory_space=pltpu.VMEM), hbm, hbm],
         out_specs=(hbm, hbm),
         out_shape=(pltpu.HBM((verts, width), bf16),) * 2,
         scratch_shapes=[
@@ -270,8 +279,8 @@
             pltpu.SemaphoreType.DMA,
             pltpu.SemaphoreType.DMA,
         ],
-        compiler_params=pltpu.CompilerParams(vmem_limit_bytes=48 * 2**20),
-    )(slot_rows, slot_cols, slots, dz, weight_t, tiles)
+        compiler_params=pltpu.CompilerParams(vmem_limit_bytes=49 * 2**20),
+    )(table, dz, weight_t, tiles)
 
 
 def terms_kernel(left_hbm, right_hbm, out_ref, left, right, left_sem, right_sem):
@@ -332,10 +341,10 @@
     snaps, own, width = cotangent.shape
     verts = snaps * own
     dz = exchange(band_apply(band, cotangent, False)).reshape(verts, width)
-    tiles, slot_rows, slot_cols, slots, weight_t = prepare(
+    tiles, table, weight_t = prepare(
         block_rows[0, 0], block_cols[0, 0], block_counts[0], block_values[0, 0], weight[0], verts // BLK
     )
-    second, dz = two_hops(slot_rows, slot_cols, slots, dz, weight_t, tiles)
+    second, dz = two_hops(table, dz, weight_t, tiles)
     input_grad = band_apply(band, exchange(second.reshape(snaps, own, width)), True)
     terms = gradient_terms(propagated[0], dz)
     weight_grad = cluster_sum(terms, n_cluster)

time: 116 us -> 115 us (level)
  waiting for transfers between devices: 59.2 us -> 57.1 us
  Pallas kernels: 25.7 us -> 27.5 us
    all_to_all x2, waiting for transfers between devices: 43 us -> 41.1 us  [exchange(): return lax.all_to_all(field, 'tm', split_axis=0, concat_axis=0, tiled=True)]
    all_to_all x2, starting transfers between devices: 14.8 us -> 13.3 us  [exchange(): return lax.all_to_all(field, 'tm', split_axis=0, concat_axis=0, tiled=True)]
    pallas_call x1, Pallas kernels: 5.79 us -> 7.05 us  [prepare(): pl.pallas_call(prepare_kernel, in_specs=[smem, smem, smem, hbm, hbm], out...]
    unnamed x8 -> x6, local copies, waits for them, and re-layouts: 2.36 us -> 1.71 us
  transfers between devices with their start and end apart: 8 -> 8, of which waited for: 8 -> 8; matrix products, arithmetic and copies ran while one was open for 4% -> 4% of each run, Pallas kernels for 10% -> 11%
where the time goes in v5:
time: 115 us; the launch traced here: 114 us
  waiting for transfers between devices  57.1 us (50%)
  Pallas kernels  27.5 us (24%)
  starting transfers between devices  21.6 us (19%)
  local copies, waits for them, and re-layouts  3.52 us (3%)
  other arithmetic  3.11 us (3%)
  between operations  1.56 us (1%)
    all_to_all x2, waiting for transfers between devices, exchange(): return lax.all_to_all(field, 'tm', split_axis=0, concat_axis=0, tiled=True)  41.1 us
    ppermute x6, waiting for transfers between devices, shift(): return lax.ppermute(array, 'cluster', [(i, (i + k) % n) for i in range(n)])  16 us
    all_to_all x2, starting transfers between devices, exchange(): return lax.all_to_all(field, 'tm', split_axis=0, concat_axis=0, tiled=True)  13.3 us
    ppermute x6, starting transfers between devices, shift(): return lax.ppermute(array, 'cluster', [(i, (i + k) % n) for i in range(n)])  8.3 us
    pallas_call x2, Pallas kernels, band_apply(): pl.pallas_call(functools.partial(band_kernel if resident else band_pull_k...  7.64 us
    pallas_call x1, Pallas kernels, two_hops(): pl.pallas_call(hops_kernel, in_specs=[smem, pl.BlockSpec(memory_space=plt...  7.33 us
    pallas_call x1, Pallas kernels, prepare(): pl.pallas_call(prepare_kernel, in_specs=[smem, smem, smem, hbm, hbm], out...  7.05 us
    pallas_call x1, Pallas kernels, gradient_terms(): pl.pallas_call(terms_kernel, in_specs=[hbm, hbm], out_specs=pl.BlockSpec(...  5.47 us
  transfers between devices with their start and end apart: 8, of which 8 were waited for; matrix products, arithmetic and copies ran while one was open for 4% of the time, Pallas kernels for 11%

profile of v5, /device:TPU:0, one launch (start us, length us, event | category | flops | bytes accessed | tf_op | source)
XLA Modules:
  0.0 114.3 jit_solution(760273440562074386)
XLA Ops:
  0.6 4.5 %shard_map.96 = bf16[32,96,512]{2,1,0:T(8,128)(2,1)} custom-call(s32[32]{0:T(128)} %band_ref.3, bf16[32,96,512]{2,1,0:T(8,128)(2,1)} %field_hbm.1), custom_call_target="tpu_custom_call" | custom-call | tf_op jit(solution)/shard_map/pallas_call | solution.py:83
  5.1 7.4 %all-to-all-start = ((bf16[32,96,512]{2,1,0:T(8,128)(2,1)}), bf16[32,96,512]{2,1,0:T(8,128)(2,1)S(1)}, u32[]{:S(2)}, u32[]{:S(2)}) async-start(bf16[32,96,512]{2,1,0:T(8,128)(2,1)} %shard_map.96), calls=%async_computation | async-start | bytes 6291456 | tf_op jit(solution)/shard_map/all_to_all | solution.py:316
  13.2 7.1 %shard_map.95 = (bf16[160,128,128]{2,1,0:T(8,128)(2,1)}, s32[241]{0:T(256)}, bf16[512,512]{1,0:T(8,128)(2,1)}) custom-call(s32[128]{0:T(128)} %bitcast.33, s32[128]{0:T(128)} %bitcast.34, s32[1]{0:T(128)} %bitcast.22.count_ref, bf16[128,128,128]{2,1,0:T(8,128)(2,1)} %bitcast.24, bf16[512,512]{1,0:T(8,128)(2,1)} %bitcast.30), custom_call_target="tpu_custom_call" | custom-call | tf_op jit(solution)/shard_map/pallas_call | solution.py:159
  20.3 34.1 %all-to-all-done = bf16[32,96,512]{2,1,0:T(8,128)(2,1)S(1)} async-done(((bf16[32,96,512]{2,1,0:T(8,128)(2,1)}), bf16[32,96,512]{2,1,0:T(8,128)(2,1)S(1)}, u32[]{:S(2)}, u32[]{:S(2)}) %all-to-all-start) | async-done | bytes 3145760 | tf_op jit(solution)/shard_map/all_to_all | solution.py:316
  54.3 0.0 copy-start
  54.3 1.0 copy-done
  55.4 0.0 copy-start.2
  55.4 0.7 copy-done.2
  56.0 7.3 %shard_map.97 = (bf16[3072,512]{1,0:T(8,128)(2,1)}, bf16[3072,512]{1,0:T(8,128)(2,1)}) custom-call(s32[241]{0:T(256)S(1)} %copy-done.2, bf16[3072,512]{1,0:T(8,128)(2,1)S(1)} %bitcast.23, bf16[512,512]{1,0:T(8,128)(2,1)S(1)} %copy-done, bf16[160,128,128]{2,1,0:T(8,128)(2,1)} %get-tuple-element.9.tiles_hbm), custom_call_target="tpu_custom_call" | custom-call | tf_op jit(solution)/shard_map/pallas_call | solution.py:265
  63.4 5.9 %all-to-all-start.1 = ((bf16[32,96,512]{2,1,0:T(8,128)(2,1)}), bf16[32,96,512]{2,1,0:T(8,128)(2,1)S(1)}, u32[]{:S(2)}, u32[]{:S(2)}) async-start(bf16[32,96,512]{2,1,0:T(8,128)(2,1)} %bitcast.25), calls=%async_computation.1 | async-start | bytes 6291456 | tf_op jit(solution)/shard_map/all_to_all | solution.py:316
  69.3 5.5 %shard_map.99 = bf16[512,512]{1,0:T(8,128)(2,1)} custom-call(bf16[3072,512]{1,0:T(8,128)(2,1)} %bitcast.26, bf16[3072,512]{1,0:T(8,128)(2,1)} %get-tuple-element.11.right_hbm), custom_call_target="tpu_custom_call" | custom-call | tf_op jit(solution)/shard_map/pallas_call | solution.py:300
  74.8 0.0 copy-start.1
  74.8 1.8 %dynamic-slice_bitcast_fusion.2 = (bf16[128,512]{1,0:T(8,128)(2,1)S(1)}, bf16[128,512]{1,0:T(8,128)(2,1)}, bf16[128,512]{1,0:T(8,128)(2,1)}) fusion(bf16[4,128,512]{2,1,0:T(8,128)(2,1)} %bitcast.27, s32[]{:T(128)S(6)} %select_n.51, s32[]{:T(128)S(6)} %select_n.55, s32[]{:T(128)S(6)} %select_n.53), kind=kLoop, calls=%fused_computation.8 | loop fusion | bytes 786444 | tf_op jit(solution)/shard_map/jit(dynamic_index_in_dim)/squeeze | solution.py:327
  76.5 4.1 %collective-permute-start.2 = (bf16[128,512]{1,0:T(8,128)(2,1)}, bf16[128,512]{1,0:T(8,128)(2,1)S(1)}, u32[]{:S(2)}, u32[]{:S(2)}) collective-permute-start(bf16[128,512]{1,0:T(8,128)(2,1)} %get-tuple-element.17), channel_id=1, source_target_pairs={{0,3},{1,0},{2,1},{3,2},{4,7},{5,4},{6,5},{7,6},{8,11},{9,8},{10,9... | collective-permute-start | bytes 393224 | tf_op jit(solution)/shard_map/ppermute | solution.py:324
  80.6 1.0 collective-permute-start.1
  81.6 0.5 collective-permute-start
  82.1 4.8 %collective-permute-done.2 = bf16[128,512]{1,0:T(8,128)(2,1)S(1)} collective-permute-done((bf16[128,512]{1,0:T(8,128)(2,1)}, bf16[128,512]{1,0:T(8,128)(2,1)S(1)}, u32[]{:S(2)}, u32[]{:S(2)}) %collective-permute-start.2) | collective-permute-done | bytes 131104 | tf_op jit(solution)/shard_map/ppermute | solution.py:324
  87.0 1.7 %collective-permute-done.1 = bf16[128,512]{1,0:T(8,128)(2,1)S(1)} collective-permute-done((bf16[128,512]{1,0:T(8,128)(2,1)}, bf16[128,512]{1,0:T(8,128)(2,1)S(1)}, u32[]{:S(2)}, u32[]{:S(2)}) %collective-permute-start.1) | collective-permute-done | bytes 131104 | tf_op jit(solution)/shard_map/ppermute | solution.py:324
  88.7 1.9 %collective-permute-done = bf16[128,512]{1,0:T(8,128)(2,1)} collective-permute-done((bf16[128,512]{1,0:T(8,128)(2,1)S(1)}, bf16[128,512]{1,0:T(8,128)(2,1)}, u32[]{:S(2)}, u32[]{:S(2)}) %collective-permute-start) | collective-permute-done | bytes 131104 | tf_op jit(solution)/shard_map/ppermute | solution.py:324
  90.6 1.0 fusion.2
  91.7 0.8 collective-permute-start.5
  92.5 1.0 collective-permute-start.4
  93.5 0.9 collective-permute-start.3
  94.4 3.9 %collective-permute-done.5 = bf16[128,512]{1,0:T(8,128)(2,1)S(1)} collective-permute-done((bf16[128,512]{1,0:T(8,128)(2,1)S(1)}, bf16[128,512]{1,0:T(8,128)(2,1)S(1)}, u32[]{:S(2)}, u32[]{:S(2)}) %collective-permute-start.5) | collective-permute-done | bytes 131104 | tf_op jit(solution)/shard_map/ppermute | solution.py:324
  98.3 1.6 %collective-permute-done.4 = bf16[128,512]{1,0:T(8,128)(2,1)S(1)} collective-permute-done((bf16[128,512]{1,0:T(8,128)(2,1)S(1)}, bf16[128,512]{1,0:T(8,128)(2,1)S(1)}, u32[]{:S(2)}, u32[]{:S(2)}) %collective-permute-start.4) | collective-permute-done | bytes 131104 | tf_op jit(solution)/shard_map/ppermute | solution.py:324
  99.9 2.0 %collective-permute-done.3 = bf16[128,512]{1,0:T(8,128)(2,1)} collective-permute-done((bf16[128,512]{1,0:T(8,128)(2,1)S(1)}, bf16[128,512]{1,0:T(8,128)(2,1)}, u32[]{:S(2)}, u32[]{:S(2)}) %collective-permute-start.3) | collective-permute-done | bytes 131104 | tf_op jit(solution)/shard_map/ppermute | solution.py:324
  101.9 1.0 pad_maximum_fusion
  102.9 1.1 maximum_convert_fusion
  104.0 7.0 %all-to-all-done.1.field = bf16[32,96,512]{2,1,0:T(8,128)(2,1)S(1)} async-done(((bf16[32,96,512]{2,1,0:T(8,128)(2,1)}), bf16[32,96,512]{2,1,0:T(8,128)(2,1)S(1)}, u32[]{:S(2)}, u32[]{:S(2)}) %all-to-all-start.1) | async-done | bytes 3145760 | tf_op jit(solution)/shard_map/all_to_all | solution.py:316
  111.0 0.0 copy-done.1
  111.0 3.2 %shard_map.98 = bf16[32,96,512]{2,1,0:T(8,128)(2,1)} custom-call(s32[32]{0:T(128)S(1)} %copy-done.1, bf16[32,96,512]{2,1,0:T(8,128)(2,1)S(1)} %all-to-all-done.1.field), custom_call_target="tpu_custom_call" | custom-call | tf_op jit(solution)/shard_map/pallas_call | solution.py:83
  (1 shorter events, 0.0 us)
Async XLA Ops:
  5.1 49.2 %all-to-all-start = ((bf16[32,96,512]{2,1,0:T(8,128)(2,1)}), bf16[32,96,512]{2,1,0:T(8,128)(2,1)S(1)}, u32[]{:S(2)}, u32[]{:S(2)}) async-start(bf16[32,96,512]{2,1,0:T(8,128)(2,1)} %shard_map.96), calls=%async_computation | async-start | bytes 6291456 | tf_op jit(solution)/shard_map/all_to_all | solution.py:316
  54.3 1.0 copy-start
  55.4 0.7 copy-start.2
  63.4 47.6 %all-to-all-start.1 = ((bf16[32,96,512]{2,1,0:T(8,128)(2,1)}), bf16[32,96,512]{2,1,0:T(8,128)(2,1)S(1)}, u32[]{:S(2)}, u32[]{:S(2)}) async-start(bf16[32,96,512]{2,1,0:T(8,128)(2,1)} %bitcast.25), calls=%async_computation.1 | async-start | bytes 6291456 | tf_op jit(solution)/shard_map/all_to_all | solution.py:316
  74.8 36.2 %copy-start.1 = (s32[32]{0:T(128)S(1)}, s32[32]{0:T(128)}, u32[]{:S(2)}) copy-start(s32[32]{0:T(128)} %band_ref.3) | copy-start | bytes 388
  76.5 10.4 %collective-permute-start.2 = (bf16[128,512]{1,0:T(8,128)(2,1)}, bf16[128,512]{1,0:T(8,128)(2,1)S(1)}, u32[]{:S(2)}, u32[]{:S(2)}) collective-permute-start(bf16[128,512]{1,0:T(8,128)(2,1)} %get-tuple-element.17), channel_id=1, source_target_pairs={{0,3},{1,0},{2,1},{3,2},{4,7},{5,4},{6,5},{7,6},{8,11},{9,8},{10,9... | collective-permute-start | bytes 393224 | tf_op jit(solution)/shard_map/ppermute | solution.py:324
  80.6 8.1 %collective-permute-start.1 = (bf16[128,512]{1,0:T(8,128)(2,1)}, bf16[128,512]{1,0:T(8,128)(2,1)S(1)}, u32[]{:S(2)}, u32[]{:S(2)}) collective-permute-start(bf16[128,512]{1,0:T(8,128)(2,1)} %get-tuple-element.18), channel_id=1, source_target_pairs={{0,2},{1,3},{2,0},{3,1},{4,6},{5,7},{6,4},{7,5},{8,10},{9,11},{10,... | collective-permute-start | bytes 393224 | tf_op jit(solution)/shard_map/ppermute | solution.py:324
  81.6 9.0 %collective-permute-start = (bf16[128,512]{1,0:T(8,128)(2,1)S(1)}, bf16[128,512]{1,0:T(8,128)(2,1)}, u32[]{:S(2)}, u32[]{:S(2)}) collective-permute-start(bf16[128,512]{1,0:T(8,128)(2,1)S(1)} %get-tuple-element.16), channel_id=1, source_target_pairs={{0,1},{1,2},{2,3},{3,0},{4,5},{5,6},{6,7},{7,4},{8,9},{9,10},{10,1... | collective-permute-start | bytes 393224 | tf_op jit(solution)/shard_map/ppermute | solution.py:324
  91.7 6.6 %collective-permute-start.5 = (bf16[128,512]{1,0:T(8,128)(2,1)S(1)}, bf16[128,512]{1,0:T(8,128)(2,1)S(1)}, u32[]{:S(2)}, u32[]{:S(2)}) collective-permute-start(bf16[128,512]{1,0:T(8,128)(2,1)S(1)} %fusion.2), channel_id=1, source_target_pairs={{0,3},{1,0},{2,1},{3,2},{4,7},{5,4},{6,5},{7,6},{8,11},{9,8},{10,9... | collective-permute-start | bytes 393224 | tf_op jit(solution)/shard_map/ppermute | solution.py:324
  92.5 7.4 %collective-permute-start.4 = (bf16[128,512]{1,0:T(8,128)(2,1)S(1)}, bf16[128,512]{1,0:T(8,128)(2,1)S(1)}, u32[]{:S(2)}, u32[]{:S(2)}) collective-permute-start(bf16[128,512]{1,0:T(8,128)(2,1)S(1)} %fusion.2), channel_id=1, source_target_pairs={{0,2},{1,3},{2,0},{3,1},{4,6},{5,7},{6,4},{7,5},{8,10},{9,11},{10,... | collective-permute-start | bytes 393224 | tf_op jit(solution)/shard_map/ppermute | solution.py:324
  93.5 8.3 %collective-permute-start.3 = (bf16[128,512]{1,0:T(8,128)(2,1)S(1)}, bf16[128,512]{1,0:T(8,128)(2,1)}, u32[]{:S(2)}, u32[]{:S(2)}) collective-permute-start(bf16[128,512]{1,0:T(8,128)(2,1)S(1)} %fusion.2), channel_id=1, source_target_pairs={{0,1},{1,2},{2,3},{3,0},{4,5},{5,6},{6,7},{7,4},{8,9},{9,10},{10,1... | collective-permute-start | bytes 393224 | tf_op jit(solution)/shard_map/ppermute | solution.py:324
